TPU v7x, 512 devices: a whole 4x8x8 slice. The times are simulated.
512 devices in a mesh: src: 16 (over y, core), tgt: 32 (over x, z).
Axes of the slice: x: 4, y: 8, z: 8, core: 2. Of those that a mesh axis runs over, the one named last changes fastest.
Arguments:
- src_centroids: bfloat16 [64, 16384], P(None, 'src')
- tgt_centroids: bfloat16 [64, 16384], P(None, 'tgt')
- src_weights: float32 [16384], P('src'), may hold values from -3 to 3
- tgt_weights: float32 [16384], P('tgt'), may hold values from -3 to 3
- src_cells: bfloat16 [64, 131072], P(None, 'src')
- tgt_cells: bfloat16 [64, 65536], P(None, 'tgt')
- src_mass: float32 [131072], P('src'), may hold values from -3 to 3
- tgt_mass: float32 [65536], P('tgt'), may hold values from -3 to 3
- src_cluster: int32 [131072], P('src'), may hold values from 0 to 16383
- tgt_cluster: int32 [65536], P('tgt'), may hold values from 0 to 16383
- support: int32 [512, 32, 4], P('src', 'tgt'), may hold values from 0 to 7, as said below
- counts: int32 [512, 32], P('src', 'tgt'), may hold values from 1 to 4, as said below
Outputs:
- fine_src: float32 [131072], P('src')
- fine_tgt: float32 [65536], P('tgt')
Inputs may be any that keep to these rules, and one draw needn't show every extreme that they name: support[b, t, m] is a tile number local to target shard t; the entries with m < counts[b, t] are distinct, later entries are ignored; for every source shard and target shard, the live entries of the shard's 32 source blocks name every one of the 8 local tiles. `counts`: for every source shard and target shard, some block of the source shard has 4 live entries.
All inputs are finite; a program needn't handle non-finite values.
Results may differ from a plain program's by a relative error of at most 0.0003.
Values sent between devices are 32-bit elements; how exact they have to be, the bound alone decides.
No kernel may reach another device: no remote copies, remote signals or barrier semaphores. Data moves between devices by JAX's collectives and lax.ppermute only.
A program may use at most 64 MiB of HBM per device.

v0:
```python
import jax
import jax.numpy as jnp
from jax import lax
from jax.sharding import PartitionSpec as P

TILE = 256
COARSE_IT = 2
FINE_IT = 2


entropy_scale = 0.0625
very_low = -1e30
blocks_per_turn = 4


def squared_norms(points):
    wide = points.astype(jnp.float32)
    return jnp.sum(wide * wide, axis=0)


def coarse_row_lse(peak, total):
    highest = lax.pmax(peak, "tgt")
    total = lax.psum(total * jnp.exp(peak - highest), "tgt")
    peak = highest
    return peak + jnp.log(total)


def coarse_col_lse(peak, total):
    highest = lax.pmax(peak, "src")
    total = lax.psum(total * jnp.exp(peak - highest), "src")
    peak = highest
    return peak + jnp.log(total)


def fine_row_lse(peak, total):
    highest = lax.pmax(peak, "tgt")
    total = lax.psum(total * jnp.exp(peak - highest), "tgt")
    peak = highest
    return peak + jnp.log(total)


def fine_col_lse(peak, total):
    highest = lax.pmax(peak, "src")
    total = lax.psum(total * jnp.exp(peak - highest), "src")
    peak = highest
    return peak + jnp.log(total)


def coarse_level(src_centroids, tgt_centroids, src_weights, tgt_weights):
    embed_dim = src_centroids.shape[0]
    inner = jnp.einsum(
        "ex,ey->xy", src_centroids, tgt_centroids, preferred_element_type=jnp.float32
    )
    cost = (
        squared_norms(src_centroids)[:, None] + squared_norms(tgt_centroids)[None, :] - 2.0 * inner
    ) / (2.0 * embed_dim)
    coarse_src = jnp.zeros(src_weights.shape, jnp.float32)
    coarse_tgt = jnp.zeros(tgt_weights.shape, jnp.float32)
    for iteration in range(COARSE_IT):
        rows = tgt_weights[None, :] + (coarse_tgt[None, :] - cost) / entropy_scale
        row_peak = jnp.max(rows, axis=1)
        row_total = jnp.sum(jnp.exp(rows - row_peak[:, None]), axis=1)
        cols = src_weights[:, None] + (coarse_src[:, None] - cost) / entropy_scale
        col_peak = jnp.max(cols, axis=0)
        col_total = jnp.sum(jnp.exp(cols - col_peak[None, :]), axis=0)
        row_new = -entropy_scale * coarse_row_lse(row_peak, row_total)
        col_new = -entropy_scale * coarse_col_lse(col_peak, col_total)
        coarse_src = 0.5 * (coarse_src + row_new)
        coarse_tgt = 0.5 * (coarse_tgt + col_new)
    return (coarse_src, coarse_tgt)


def fold_pairs(peak, total, part_peak, part_total, owner, slots):
    match = owner[:, None] == jnp.arange(slots, dtype=jnp.int32)[None, :]
    spread_peak = jnp.where(match[:, :, None], part_peak[:, None, :], very_low)
    new_peak = jnp.maximum(peak, jnp.max(spread_peak, axis=0))
    scaled = jnp.where(
        match[:, :, None], part_total[:, None, :] * jnp.exp(spread_peak - new_peak[None, :, :]), 0.0
    )
    new_total = total * jnp.exp(peak - new_peak) + jnp.sum(scaled, axis=0)
    return (new_peak, new_total)


def fine_level(src_cells, tgt_cells, src_mass, tgt_mass, support, counts, fine_src, fine_tgt):
    embed_dim = src_cells.shape[0]
    blocks = src_cells.shape[1] // TILE
    tile_count = tgt_cells.shape[1] // TILE
    list_len = support.shape[2]
    pair_count = blocks * list_len
    pair_group = blocks_per_turn * list_len
    src_tiles = src_cells.reshape(embed_dim, blocks, TILE)
    tgt_tiles = tgt_cells.reshape(embed_dim, tile_count, TILE)
    src_norm = squared_norms(src_cells).reshape(blocks, TILE)
    tgt_norm = squared_norms(tgt_cells).reshape(tile_count, TILE)
    src_weight = src_mass.reshape(blocks, TILE)
    tgt_weight = tgt_mass.reshape(tile_count, TILE)
    pair_index = jnp.arange(pair_count, dtype=jnp.int32)
    pair_block = pair_index // list_len
    pair_tile = support.reshape(pair_count)
    pair_live = pair_index % list_len < counts.reshape(blocks)[pair_block]
    turn_count = blocks // blocks_per_turn
    for iteration in range(FINE_IT):
        src_pot = fine_src.reshape(blocks, TILE)
        tgt_pot = fine_tgt.reshape(tile_count, TILE)

        def padded_turn(turn, carry):
            row_peak, row_total, col_peak, col_total = carry
            first_block = turn * blocks_per_turn
            first_pair = turn * pair_group
            which_tile = lax.dynamic_slice_in_dim(pair_tile, first_pair, pair_group)
            which_live = lax.dynamic_slice_in_dim(pair_live, first_pair, pair_group)
            live_grid = which_live.reshape(blocks_per_turn, list_len)
            left = lax.dynamic_slice_in_dim(src_tiles, first_block, blocks_per_turn, 1)
            right = tgt_tiles[:, which_tile].reshape(embed_dim, blocks_per_turn, list_len, TILE)
            inner = jnp.einsum("ebx,ebmy->bmxy", left, right, preferred_element_type=jnp.float32)
            left_norm = lax.dynamic_slice_in_dim(src_norm, first_block, blocks_per_turn, 0)
            right_norm = tgt_norm[which_tile].reshape(blocks_per_turn, list_len, TILE)
            cost = (left_norm[:, None, :, None] + right_norm[:, :, None, :] - 2.0 * inner) / (
                2.0 * embed_dim
            )
            right_weight = tgt_weight[which_tile].reshape(blocks_per_turn, list_len, TILE)
            right_pot = tgt_pot[which_tile].reshape(blocks_per_turn, list_len, TILE)
            rows = right_weight[:, :, None, :] + (right_pot[:, :, None, :] - cost) / entropy_scale
            rows = jnp.where(live_grid[:, :, None, None], rows, very_low)
            block_peak = jnp.max(rows, axis=(1, 3))
            block_total = jnp.sum(jnp.exp(rows - block_peak[:, None, :, None]), axis=(1, 3))
            row_peak = lax.dynamic_update_slice_in_dim(row_peak, block_peak, first_block, 0)
            row_total = lax.dynamic_update_slice_in_dim(row_total, block_total, first_block, 0)
            left_weight = lax.dynamic_slice_in_dim(src_weight, first_block, blocks_per_turn, 0)
            left_pot = lax.dynamic_slice_in_dim(src_pot, first_block, blocks_per_turn, 0)
            cols = (
                left_weight[:, None, :, None] + (left_pot[:, None, :, None] - cost) / entropy_scale
            )
            part_peak = jnp.max(cols, axis=2)
            part_total = jnp.sum(jnp.exp(cols - part_peak[:, :, None, :]), axis=2)
            part_peak = jnp.where(live_grid[:, :, None], part_peak, very_low).reshape(
                pair_group, TILE
            )
            part_total = jnp.where(live_grid[:, :, None], part_total, 0.0).reshape(pair_group, TILE)
            col_peak, col_total = fold_pairs(
                col_peak, col_total, part_peak, part_total, which_tile, tile_count
            )
            return (row_peak, row_total, col_peak, col_total)

        start_carry = (
            jnp.full((blocks, TILE), very_low, jnp.float32),
            jnp.zeros((blocks, TILE), jnp.float32),
            jnp.full((tile_count, TILE), very_low, jnp.float32),
            jnp.zeros((tile_count, TILE), jnp.float32),
        )
        row_peak, row_total, col_peak, col_total = lax.fori_loop(
            0, turn_count, padded_turn, start_carry
        )
        row_new = -entropy_scale * fine_row_lse(
            row_peak.reshape(blocks * TILE), row_total.reshape(blocks * TILE)
        )
        col_new = -entropy_scale * fine_col_lse(
            col_peak.reshape(tile_count * TILE), col_total.reshape(tile_count * TILE)
        )
        fine_src = 0.5 * (fine_src + row_new)
        fine_tgt = 0.5 * (fine_tgt + col_new)
    return (fine_src, fine_tgt)


def per_device(
    src_centroids,
    tgt_centroids,
    src_weights,
    tgt_weights,
    src_cells,
    tgt_cells,
    src_mass,
    tgt_mass,
    src_cluster,
    tgt_cluster,
    support,
    counts,
):
    coarse_src, coarse_tgt = coarse_level(src_centroids, tgt_centroids, src_weights, tgt_weights)
    every_src = lax.all_gather(coarse_src, "src", axis=0, tiled=True)
    every_tgt = lax.all_gather(coarse_tgt, "tgt", axis=0, tiled=True)
    fine_src = every_src[src_cluster]
    fine_tgt = every_tgt[tgt_cluster]
    return fine_level(src_cells, tgt_cells, src_mass, tgt_mass, support, counts, fine_src, fine_tgt)


def solution(mesh):
    in_specs = (
        P(None, "src"),
        P(None, "tgt"),
        P("src"),
        P("tgt"),
        P(None, "src"),
        P(None, "tgt"),
        P("src"),
        P("tgt"),
        P("src"),
        P("tgt"),
        P("src", "tgt", None),
        P("src", "tgt"),
    )
    out_specs = (P("src"), P("tgt"))
    return jax.shard_map(
        per_device, mesh=mesh, in_specs=in_specs, out_specs=out_specs, check_vma=False
    )
```

profile of v0, /device:TPU:32, one launch (start us, length us, event | category | flops | bytes accessed | tf_op | source)
XLA Modules:
  0.0 1269.7 jit_solution(3313173037689012017)
XLA Ops:
  0.7 1.0 multiply_reduce_fusion.2
  1.6 0.9 multiply_reduce_fusion.3
  2.5 1.8 add_reduce_fusion.1
  4.3 0.7 exponential_reduce_fusion.7
  4.9 80.9 %pmax.56 = f32[1024]{0:T(1024)S(1)} all-reduce(f32[1024]{0:T(1024)S(1)} %get-tuple-element.810), channel_id=1, replica_groups=mesh['src'=16,'tgt'=32] {'tgt'}, use_global_device_ids=true, to_apply=%region_3.0 | all-reduce | flops 1024 | bytes 8192 | tf_op jit(solution)/shard_map/pmax | solution.py:22
  85.8 69.6 %psum.56 = f32[1024]{0:T(1024)S(1)} all-reduce(f32[1024]{0:T(1024)S(1)} %exponential_multiply_fusion.5), channel_id=1, replica_groups=mesh['src'=16,'tgt'=32] {'tgt'}, use_global_device_ids=true, to_apply=%region_5.0 | all-reduce | flops 1024 | bytes 8192 | tf_op jit(solution)/shard_map/psum | solution.py:23
  155.8 0.8 exponential_reduce_fusion.4
  156.6 23.6 %all-reduce.1 = (f32[512]{0:T(512)S(1)}, f32[512]{0:T(512)S(1)}) all-reduce(f32[512]{0:T(512)S(1)} %get-tuple-element.729, f32[512]{0:T(512)S(1)} %fusion.23), channel_id=1, replica_groups=mesh['src'=16,'tgt'=32] {'src'}, use_global_device_ids=true, to_apply=%region_7.0 | all-reduce | flops 1024 | bytes 8192 | tf_op jit(solution)/shard_map/pmax | solution.py:29
  180.7 23.6 %all-reduce = (f32[512]{0:T(512)S(1)}, f32[512]{0:T(512)S(1)}) all-reduce(f32[512]{0:T(512)S(1)} %get-tuple-element.813, f32[512]{0:T(512)S(1)} %get-tuple-element.812), channel_id=1, replica_groups=mesh['src'=16,'tgt'=32] {'src'}, use_global_device_ids=true, to_apply=%region_9.0 | all-reduce | flops 1024 | bytes 8192 | tf_op jit(solution)/shard_map/psum | solution.py:30
  204.7 0.7 exponential_reduce_fusion.5
  205.3 71.6 %pmax.58 = f32[1024]{0:T(1024)S(1)} all-reduce(f32[1024]{0:T(1024)S(1)} %fusion.22), channel_id=1, replica_groups=mesh['src'=16,'tgt'=32] {'tgt'}, use_global_device_ids=true, to_apply=%region_11.0 | all-reduce | flops 1024 | bytes 8192 | tf_op jit(solution)/shard_map/pmax | solution.py:22
  277.0 69.6 %psum.58 = f32[1024]{0:T(1024)S(1)} all-reduce(f32[1024]{0:T(1024)S(1)} %exponential_multiply_fusion.4), channel_id=1, replica_groups=mesh['src'=16,'tgt'=32] {'tgt'}, use_global_device_ids=true, to_apply=%region_13.0 | all-reduce | flops 1024 | bytes 8192 | tf_op jit(solution)/shard_map/psum | solution.py:23
  346.6 14.3 %all_gather.6 = f32[16384]{0:T(1024)S(1)} all-gather(f32[1024]{0:T(1024)S(1)} %add_multiply_fusion.4), channel_id=1, replica_groups=mesh['src'=16,'tgt'=32] {'src'}, dimensions={0}, use_global_device_ids=true | all-gather | bytes 69632 | tf_op jit(solution)/shard_map/all_gather | solution.py:180
  361.0 45.5 %gather_fusion.8 = f32[8192]{0:T(1024)S(1)} fusion(f32[16384]{0:T(1024)S(1)} %all_gather.6, s32[8192]{0:T(1024)S(1)} %fusion.24), kind=kCustom, calls=%fused_computation.8 | custom fusion | bytes 98304 | tf_op jit(solution)/shard_map/gather | solution.py:182
  406.5 47.5 %all-gather = f32[32,1,512]{2,1,0:T(1,128)S(1)} all-gather(f32[1,1,512]{2,1,0:T(1,128)S(1)} %bitcast.103), channel_id=1, replica_groups=mesh['src'=16,'tgt'=32] {'tgt'}, dimensions={0}, use_global_device_ids=true | all-gather | bytes 67584 | tf_op jit(solution)/shard_map/all_gather | solution.py:181
  454.1 11.8 gather_fusion.10
  466.7 1.2 gather_fusion.9
  468.0 75.1 %while.40 = (s32[]{:T(128)}, f32[32,256]{1,0:T(8,128)S(1)}, f32[32,256]{1,0:T(8,128)S(1)}, f32[8,256]{1,0:T(8,128)S(1)}, f32[8,256]{1,0:T(8,128)S(1)}, /*index=5...) while((s32[]{:T(128)}, f32[32,256]{1,0:T(8,128)S(1)}, ...), condition=%wide.region_27.28_spmd.clone, body=%wide.region_20.27_spmd.clone.sunk | while | flops 159622336 | bytes 10786656 | solution.py:151
  469.3 0.6 gather_fusion.2
  470.7 3.2 fusion.41
  473.9 3.0 exponential_reduce_fusion.10
  480.1 3.2 fusion.41
  483.3 3.0 exponential_reduce_fusion.10
  488.1 0.6 gather_fusion.2
  489.5 3.2 fusion.41
  492.7 3.0 exponential_reduce_fusion.10
  497.5 0.6 gather_fusion.2
  498.9 3.2 fusion.41
  502.1 3.0 exponential_reduce_fusion.10
  508.3 3.2 fusion.41
  511.5 3.0 exponential_reduce_fusion.10
  517.7 3.2 fusion.41
  520.9 3.0 exponential_reduce_fusion.10
  527.1 3.2 fusion.41
  530.3 3.0 exponential_reduce_fusion.10
  536.5 3.2 fusion.41
  539.7 3.0 exponential_reduce_fusion.10
  543.2 24.1 %pmax.61 = f32[2048]{0:T(1024)S(1)} all-reduce(f32[2048]{0:T(1024)S(1)} %bitcast.97), channel_id=1, replica_groups=mesh['src'=16,'tgt'=32] {'src'}, use_global_device_ids=true, to_apply=%region_30.31 | all-reduce | flops 2048 | bytes 16384 | tf_op jit(solution)/shard_map/pmax | solution.py:43
  567.3 24.1 %psum.61 = f32[2048]{0:T(1024)S(1)} all-reduce(f32[2048]{0:T(1024)S(1)} %exponential_multiply_fusion.3), channel_id=1, replica_groups=mesh['src'=16,'tgt'=32] {'src'}, use_global_device_ids=true, to_apply=%region_31.32 | all-reduce | flops 2048 | bytes 16384 | tf_op jit(solution)/shard_map/psum | solution.py:44
  591.4 140.3 %pmax.60 = f32[8192]{0:T(1024)S(1)} all-reduce(f32[8192]{0:T(1024)S(1)} %bitcast.85), channel_id=1, replica_groups=mesh['src'=16,'tgt'=32] {'tgt'}, use_global_device_ids=true, to_apply=%region_28.29 | all-reduce | flops 8192 | bytes 65536 | tf_op jit(solution)/shard_map/pmax | solution.py:36
  731.8 137.9 %psum.60 = f32[8192]{0:T(1024)S(1)} all-reduce(f32[8192]{0:T(1024)S(1)} %exponential_multiply_fusion.1), channel_id=1, replica_groups=mesh['src'=16,'tgt'=32] {'tgt'}, use_global_device_ids=true, to_apply=%region_29.30 | all-reduce | flops 8192 | bytes 65536 | tf_op jit(solution)/shard_map/psum | solution.py:37
  869.7 75.1 %while.41 = (s32[]{:T(128)}, f32[32,256]{1,0:T(8,128)S(1)}, f32[32,256]{1,0:T(8,128)S(1)}, f32[8,256]{1,0:T(8,128)S(1)}, f32[8,256]{1,0:T(8,128)S(1)}, /*index=5...) while((s32[]{:T(128)}, f32[32,256]{1,0:T(8,128)S(1)}, ...), condition=%wide.region_39.40_spmd.clone, body=%wide.region_32.39_spmd.clone.sunk | while | flops 159622336 | bytes 10786656 | solution.py:151
  872.4 3.2 fusion.45
  875.6 3.0 exponential_reduce_fusion.11
  881.8 3.2 fusion.45
  885.0 3.0 exponential_reduce_fusion.11
  891.2 3.2 fusion.45
  894.4 3.0 exponential_reduce_fusion.11
  900.6 3.2 fusion.45
  903.8 3.0 exponential_reduce_fusion.11
  910.0 3.2 fusion.45
  913.2 3.0 exponential_reduce_fusion.11
  919.4 3.2 fusion.45
  922.6 3.0 exponential_reduce_fusion.11
  928.8 3.2 fusion.45
  932.0 3.0 exponential_reduce_fusion.11
  938.2 3.2 fusion.45
  941.4 3.0 exponential_reduce_fusion.11
  944.9 24.1 %pmax.63 = f32[2048]{0:T(1024)S(1)} all-reduce(f32[2048]{0:T(1024)S(1)} %bitcast.99), channel_id=1, replica_groups=mesh['src'=16,'tgt'=32] {'src'}, use_global_device_ids=true, to_apply=%region_42.43 | all-reduce | flops 2048 | bytes 16384 | tf_op jit(solution)/shard_map/pmax | solution.py:43
  969.0 24.1 %psum.63 = f32[2048]{0:T(1024)S(1)} all-reduce(f32[2048]{0:T(1024)S(1)} %exponential_multiply_fusion.2), channel_id=1, replica_groups=mesh['src'=16,'tgt'=32] {'src'}, use_global_device_ids=true, to_apply=%region_43.44 | all-reduce | flops 2048 | bytes 16384 | tf_op jit(solution)/shard_map/psum | solution.py:44
  993.1 0.6 add_multiply_fusion.2
  993.7 137.7 %pmax.62 = f32[8192]{0:T(1024)S(1)} all-reduce(f32[8192]{0:T(1024)S(1)} %bitcast.87), channel_id=1, replica_groups=mesh['src'=16,'tgt'=32] {'tgt'}, use_global_device_ids=true, to_apply=%region_40.41 | all-reduce | flops 8192 | bytes 65536 | tf_op jit(solution)/shard_map/pmax | solution.py:36
  1131.4 137.7 %psum.62 = f32[8192]{0:T(1024)S(1)} all-reduce(f32[8192]{0:T(1024)S(1)} %exponential_multiply_fusion), channel_id=1, replica_groups=mesh['src'=16,'tgt'=32] {'tgt'}, use_global_device_ids=true, to_apply=%region_41.42 | all-reduce | flops 8192 | bytes 65536 | tf_op jit(solution)/shard_map/psum | solution.py:37
  1269.1 0.6 add_multiply_fusion
  (451 shorter events, 49.1 us)
Async XLA Ops:
  0.6 466.1 %copy-start = (s32[32,1]{0,1:T(1,128)S(1)}, s32[32,1]{0,1:T(1,128)}, u32[]{:S(2)}) copy-start(s32[32,1]{0,1:T(1,128)} %param.27) | copy-start | bytes 388
  0.6 3.6 copy-start.6
  0.7 154.8 %copy-start.3 = (f32[1024]{0:T(1024)S(1)}, f32[1024]{0:T(1024)}, u32[]{:S(2)}) copy-start(f32[1024]{0:T(1024)} %param.18) | copy-start | bytes 12292
  155.8 205.1 %copy-start.4 = (s32[8192]{0:T(1024)S(1)}, s32[8192]{0:T(1024)}, u32[]{:S(2)}) copy-start(s32[8192]{0:T(1024)} %param.24) | copy-start | bytes 98308
  361.0 93.1 %copy-start.7 = (s32[2048]{0:T(1024)S(1)}, s32[2048]{0:T(1024)}, u32[]{:S(2)}) copy-start(s32[2048]{0:T(1024)} %param.25) | copy-start | bytes 24580
  454.0 11.9 copy-start.1
  454.0 12.0 copy-start.2
  454.1 12.3 copy-start.5
  454.1 12.3 copy-start.9
  454.1 12.6 copy-start.8
where the time goes:
time: 1270 us
  blocking collectives  1050 us (83%)
  local copies, waits for them, and re-layouts  100 us (8%)
  other arithmetic  62.5 us (5%)
  matrix products  52.8 us (4%)
    pmax x2, blocking collectives, fine_row_lse(): highest = lax.pmax(peak, 'tgt')  278 us
    psum x2, blocking collectives, fine_row_lse(): total = lax.psum(total * jnp.exp(peak - highest), 'tgt')  276 us
    pmax x2, blocking collectives, coarse_row_lse(): highest = lax.pmax(peak, 'tgt')  152 us
    psum x2, blocking collectives, coarse_row_lse(): total = lax.psum(total * jnp.exp(peak - highest), 'tgt')  139 us
    dot_general x16, matrix products, padded_turn(): jnp.einsum('ebx,ebmy->bmxy', left, right, preferred_element_type=jnp.floa...  51.1 us
    reduce_sum x16, other arithmetic, padded_turn(): part_total = jnp.sum(jnp.exp(cols - part_peak[:, :, None, :]), axis=2)  48.3 us
    pmax x2, blocking collectives, fine_col_lse(): highest = lax.pmax(peak, 'src')  48.1 us
    psum x2, blocking collectives, fine_col_lse(): total = lax.psum(total * jnp.exp(peak - highest), 'src')  48.1 us

commit v1 on v0

v1 whole, which is shorter than its diff:
```python
import functools
import math
import jax
import jax.numpy as jnp
from jax import lax
from jax.experimental import pallas as pl
from jax.experimental.pallas import tpu as pltpu
from jax.sharding import PartitionSpec as P

TILE = 256
LANES = 128
HALVES = TILE // LANES
UNROLL = 4

eps = 0.0625
log2e = math.log2(math.e)
ln2 = math.log(2.0)
smallest = 1e-25
largest = 1e37
very_low = -3e38

f32 = jnp.float32
bf16 = jnp.bfloat16


def norms_of(points_ref, out_ref):
    for row in range(out_ref.shape[0]):
        part = points_ref[:, row * LANES : (row + 1) * LANES].astype(f32)
        out_ref[row : row + 1, :] = jnp.sum(part * part, axis=0, keepdims=True)


def transpose_points(points_ref, out_ref):
    dim, count = points_ref.shape
    for start in range(0, count, LANES):
        part = points_ref[:, start : start + LANES].astype(f32)
        part = jnp.concatenate([part, jnp.zeros((LANES - dim, LANES), f32)], axis=0)
        out_ref[start : start + LANES, :] = part.T.astype(bf16)


def to_columns(rows, out_ref):
    for row in range(rows.shape[0]):
        spread = jnp.broadcast_to(rows[row : row + 1, :], (LANES, LANES))
        out_ref[row * LANES : (row + 1) * LANES, :] = spread.T


def combine(parts):
    peak = jnp.max(parts, axis=0)
    return peak + jnp.log(jnp.sum(jnp.exp(parts - peak[None]), axis=0))


def in_range(total):
    return jnp.logical_and(jnp.min(total) >= smallest, jnp.max(total) <= largest)


class Static:
    def __init__(self, blocks, tiles):
        self.blocks, self.tiles = blocks, tiles

    def each(self, step):
        for b in range(self.blocks):
            for k in range(self.tiles):
                step(b, k, b, k)


class Listed:
    def __init__(self, list_ref, blocks, tiles):
        self.list_ref, self.blocks, self.tiles = list_ref, blocks, tiles
        self.room = (list_ref.shape[0] - 1) // 2

    def each(self, step):
        def group(index, carry):
            for u in range(UNROLL):
                at = index * UNROLL + u
                b = self.list_ref[at]
                k = self.list_ref[self.room + at]
                step(jnp.minimum(b, self.blocks - 1), jnp.minimum(k, self.tiles - 1), b, k)
            return carry

        lax.fori_loop(0, self.list_ref[2 * self.room], group, 0)


def at(index, size):
    if isinstance(index, int):
        return pl.ds(index * size, size)
    return pl.ds(pl.multiple_of(index * size, size), size)


def inner_of(right_ref, left_ref, b, k):
    dim = left_ref.shape[0]
    return jnp.dot(
        right_ref[at(k, TILE), :][:, :dim], left_ref[:, at(b, TILE)], preferred_element_type=f32
    )


def half(x, h):
    return x[:, h * LANES : (h + 1) * LANES]


def by_eights(x, op):
    return op(x.reshape(x.shape[0] // 8, 8, x.shape[1]), axis=0)


def row_of(ref, b, h):
    return ref[pl.ds(b * HALVES + h, 1), :]


def gather_columns(acc_ref, tiles, out_ref, op):
    for k in range(tiles):
        for h in range(HALVES):
            part = acc_ref[k, h * LANES : (h + 1) * LANES, :].T
            row = k * HALVES + h
            out_ref[row : row + 1, :] = op(part, axis=0, keepdims=True)


def gather_rows(acc_ref, blocks, out_ref, op):
    for b in range(blocks):
        part = op(acc_ref[b], axis=0, keepdims=True)
        for h in range(HALVES):
            row = b * HALVES + h
            out_ref[row : row + 1, :] = half(part, h)


def col_scores(weight, pot, left_norm, right_norm, right_ref, left_ref, pairs, scr, out_ref):
    dim = left_ref.shape[0]
    scale = 1.0 / (dim * eps)
    vec_ref, vec2_ref, _, _, acc_ref, col_ref, col2_ref = scr
    terms = weight + pot * (1.0 / eps)
    alpha = (terms - left_norm * (0.5 * scale)) * log2e
    top = jnp.max(alpha, keepdims=True)
    rows = alpha.shape[0]
    vec_ref[0:rows, :] = alpha - top
    acc_ref[...] = jnp.zeros(acc_ref.shape, f32)

    def add(b, k, to_b, to_k):
        z = inner_of(right_ref, left_ref, b, k) * (scale * log2e)
        parts = [jnp.exp2(half(z, h) + row_of(vec_ref, b, h)) for h in range(HALVES)]
        acc_ref[to_k] += functools.reduce(jnp.add, parts)

    pairs.each(add)
    gather_columns(acc_ref, pairs.tiles, out_ref, jnp.sum)
    total = out_ref[...]
    out_ref[...] = jnp.log(total) + top * ln2 - right_norm * (0.5 * scale)

    @pl.when(jnp.logical_not(in_range(total)))
    def _():
        vec_ref[0:rows, :] = terms
        vec2_ref[0:rows, :] = left_norm
        to_columns(right_norm, col_ref)
        acc_ref[...] = jnp.full(acc_ref.shape, very_low, f32)

        def scores(b, k):
            z = inner_of(right_ref, left_ref, b, k)
            tgt = col_ref[at(k, TILE), :]
            for h in range(HALVES):
                cost = (row_of(vec2_ref, b, h) + tgt - 2.0 * half(z, h)) * (1.0 / (2.0 * dim))
                yield row_of(vec_ref, b, h) - cost * (1.0 / eps)

        def highest(b, k, to_b, to_k):
            acc_ref[to_k] = functools.reduce(jnp.maximum, scores(b, k), acc_ref[to_k])

        pairs.each(highest)
        gather_columns(acc_ref, pairs.tiles, out_ref, jnp.max)
        peak = out_ref[...]
        to_columns(peak, col2_ref)
        acc_ref[...] = jnp.zeros(acc_ref.shape, f32)

        def add_exact(b, k, to_b, to_k):
            peaks = col2_ref[at(k, TILE), :]
            parts = [jnp.exp(s - peaks) for s in scores(b, k)]
            acc_ref[to_k] += functools.reduce(jnp.add, parts)

        pairs.each(add_exact)
        gather_columns(acc_ref, pairs.tiles, out_ref, jnp.sum)
        out_ref[...] = peak + jnp.log(out_ref[...])


def row_scores(weight, pot, right_norm, left_norm, right_ref, left_ref, pairs, scr, out_ref):
    dim = left_ref.shape[0]
    scale = 1.0 / (dim * eps)
    vec_ref, vec2_ref, acc_ref, _, _, col_ref, col2_ref = scr
    terms = weight + pot * (1.0 / eps)
    beta = (terms - right_norm * (0.5 * scale)) * log2e
    top = jnp.max(beta, keepdims=True)
    to_columns(beta - top, col_ref)
    acc_ref[...] = jnp.zeros(acc_ref.shape, f32)

    def add(b, k, to_b, to_k):
        z = inner_of(right_ref, left_ref, b, k) * (scale * log2e)
        tgt = col_ref[at(k, TILE), :]
        for h in range(HALVES):
            part = by_eights(jnp.exp2(half(z, h) + tgt), jnp.sum)
            acc_ref[to_b, :, h * LANES : (h + 1) * LANES] += part

    pairs.each(add)
    gather_rows(acc_ref, pairs.blocks, out_ref, jnp.sum)
    total = out_ref[...]
    out_ref[...] = jnp.log(total) + top * ln2 - left_norm * (0.5 * scale)

    @pl.when(jnp.logical_not(in_range(total)))
    def _():
        rows = left_norm.shape[0]
        to_columns(terms, col_ref)
        to_columns(right_norm, col2_ref)
        vec_ref[0:rows, :] = left_norm
        acc_ref[...] = jnp.full(acc_ref.shape, very_low, f32)

        def scores(b, k):
            z = inner_of(right_ref, left_ref, b, k)
            for h in range(HALVES):
                cost = (row_of(vec_ref, b, h) + col2_ref[at(k, TILE), :] - 2.0 * half(z, h)) * (
                    1.0 / (2.0 * dim)
                )
                yield col_ref[at(k, TILE), :] - cost * (1.0 / eps)

        def highest(b, k, to_b, to_k):
            for h, s in enumerate(scores(b, k)):
                where = slice(h * LANES, (h + 1) * LANES)
                acc_ref[to_b, :, where] = jnp.maximum(
                    acc_ref[to_b, :, where], by_eights(s, jnp.max)
                )

        pairs.each(highest)
        gather_rows(acc_ref, pairs.blocks, out_ref, jnp.max)
        peak = out_ref[...]
        vec2_ref[0:rows, :] = peak
        acc_ref[...] = jnp.zeros(acc_ref.shape, f32)

        def add_exact(b, k, to_b, to_k):
            for h, s in enumerate(scores(b, k)):
                where = slice(h * LANES, (h + 1) * LANES)
                acc_ref[to_b, :, where] += by_eights(
                    jnp.exp(s - row_of(vec2_ref, b, h)), jnp.sum
                )

        pairs.each(add_exact)
        gather_rows(acc_ref, pairs.blocks, out_ref, jnp.sum)
        out_ref[...] = peak + jnp.log(out_ref[...])


def look_up(table, which, out_ref):
    table = table.T
    high = table.astype(bf16)
    rest = table - high.astype(f32)
    middle = rest.astype(bf16)
    low = (rest - middle.astype(f32)).astype(bf16)
    stack = jnp.concatenate([high, middle, low], axis=0)
    place = lax.broadcasted_iota(jnp.int32, (LANES, LANES), 0)
    for row in range(which.shape[0]):
        index = which[row : row + 1, :]
        hot = jnp.where(place == lax.shift_right_logical(index, 7), 1.0, 0.0).astype(bf16)
        found = jnp.dot(stack, hot, preferred_element_type=f32)
        value = found[:LANES] + found[LANES : 2 * LANES] + found[2 * LANES :]
        value = jnp.where(place == jnp.bitwise_and(index, LANES - 1), value, 0.0)
        out_ref[row : row + 1, :] = jnp.sum(value, axis=0, keepdims=True)


def to_all(out_ref, value, start=0):
    out_ref[:, start : start + value.shape[0], :] = jnp.broadcast_to(
        value[None], (out_ref.shape[0],) + value.shape
    )


def coarse_start(left_ref, points_ref, weight_ref, send_ref, right_ref, ln_ref, rn_ref, *scr):
    norms_of(left_ref, ln_ref)
    norms_of(points_ref, rn_ref)
    transpose_points(points_ref, right_ref)
    *scr, out_ref = scr
    pairs = Static(left_ref.shape[1] // TILE, points_ref.shape[1] // TILE)
    weight = weight_ref[...]
    pot = jnp.zeros(weight.shape, f32)
    col_scores(weight, pot, ln_ref[...], rn_ref[...], right_ref, left_ref, pairs, scr, out_ref)
    to_all(send_ref, out_ref[...])


def coarse_rows(recv_ref, left_ref, right_ref, ln_ref, rn_ref, weight_ref, send_ref, tgt_ref, *scr):
    *scr, out_ref = scr
    tgt = (-0.5 * eps) * combine(recv_ref[...])
    tgt_ref[...] = tgt
    pairs = Static(left_ref.shape[1] // TILE, right_ref.shape[0] // TILE)
    for step, pot in enumerate((jnp.zeros(tgt.shape, f32), tgt)):
        row_scores(
            weight_ref[...], pot, rn_ref[...], ln_ref[...], right_ref, left_ref, pairs, scr, out_ref
        )
        to_all(send_ref, out_ref[...], step * out_ref.shape[0])


def coarse_cols(recv_ref, left_ref, right_ref, ln_ref, rn_ref, weight_ref, send_ref, *scr):
    *scr, out_ref = scr
    lse = combine(recv_ref[...])
    rows = lse.shape[0] // 2
    first = (-0.5 * eps) * lse[:rows]
    second = 0.5 * (first - eps * lse[rows:])
    to_all(send_ref, second)
    pairs = Static(left_ref.shape[1] // TILE, right_ref.shape[0] // TILE)
    col_scores(
        weight_ref[...], first, ln_ref[...], rn_ref[...], right_ref, left_ref, pairs, scr, out_ref
    )
    to_all(send_ref, out_ref[...], rows)


def coarse_end(recv_ref, tgt_ref, send_ref):
    count = tgt_ref.shape[0]
    rows = recv_ref.shape[1] - count
    lse = combine(recv_ref[:, rows:, :])
    to_all(send_ref, 0.5 * (tgt_ref[...] - eps * lse))


def prepare(left_ref, points_ref, support_ref, counts_ref, right_ref, ln_ref, rn_ref, list_ref):
    blocks = left_ref.shape[1] // TILE
    tiles = points_ref.shape[1] // TILE
    most = support_ref.shape[2]
    room = (list_ref.shape[0] - 1) // 2

    def one_block(b, found):
        count = counts_ref[b, 0]
        for m in range(most):
            list_ref[found] = b
            list_ref[room + found] = support_ref[b, 0, m]
            found = found + jnp.where(m < count, 1, 0)
        return found

    found = lax.fori_loop(0, blocks, one_block, 0)
    for u in range(UNROLL):
        list_ref[found + u] = blocks
        list_ref[room + found + u] = tiles
    list_ref[2 * room] = lax.div(found + UNROLL - 1, UNROLL)
    norms_of(left_ref, ln_ref)
    norms_of(points_ref, rn_ref)
    transpose_points(points_ref, right_ref)


def fine_cols_first(
    list_ref, recv_ref, which_ref, left_ref, right_ref, ln_ref, rn_ref, weight_ref, send_ref, src_ref, *scr
):
    *scr, table_ref, out_ref = scr
    shards = recv_ref.shape[0]
    rows = table_ref.shape[0] // shards
    for shard in range(shards):
        table_ref[shard * rows : (shard + 1) * rows, :] = recv_ref[shard, 0:rows, :]
    look_up(table_ref[...], which_ref[...], src_ref)
    pairs = Listed(list_ref, left_ref.shape[1] // TILE, right_ref.shape[0] // TILE)
    col_scores(
        weight_ref[...], src_ref[...], ln_ref[...], rn_ref[...], right_ref, left_ref, pairs, scr, out_ref
    )
    to_all(send_ref, out_ref[...])


def fine_rows_first(
    list_ref, recv_ref, which_ref, left_ref, right_ref, ln_ref, rn_ref, weight_ref, out_ref, tgt_ref, *scr
):
    *scr, table_ref = scr
    shards = recv_ref.shape[0]
    rows = table_ref.shape[0] // shards
    for shard in range(shards):
        table_ref[shard * rows : (shard + 1) * rows, :] = recv_ref[shard]
    look_up(table_ref[...], which_ref[...], tgt_ref)
    pairs = Listed(list_ref, left_ref.shape[1] // TILE, right_ref.shape[0] // TILE)
    row_scores(
        weight_ref[...], tgt_ref[...], rn_ref[...], ln_ref[...], right_ref, left_ref, pairs, scr, out_ref
    )


def fine_rows_second(
    list_ref, recv_ref, tgt_ref, first_ref, left_ref, right_ref, ln_ref, rn_ref, weight_ref, send_ref, new_ref, *scr
):
    *scr, out_ref = scr
    new_ref[...] = 0.5 * (tgt_ref[...] - eps * combine(recv_ref[...]))
    pairs = Listed(list_ref, left_ref.shape[1] // TILE, right_ref.shape[0] // TILE)
    row_scores(
        weight_ref[...], new_ref[...], rn_ref[...], ln_ref[...], right_ref, left_ref, pairs, scr, out_ref
    )
    shards, rows, _ = send_ref.shape
    rows = rows // 2
    for shard in range(shards):
        where = slice(shard * rows, (shard + 1) * rows)
        send_ref[shard, 0:rows, :] = first_ref[where, :]
        send_ref[shard, rows : 2 * rows, :] = out_ref[where, :]


def combine_rows(recv_ref, send_ref):
    to_all(send_ref, combine(recv_ref[...]))


def fine_cols_second(
    list_ref, recv_ref, src_ref, left_ref, right_ref, ln_ref, rn_ref, weight_ref, send_ref, new_ref, *scr
):
    *scr, first_ref, out_ref = scr
    shards, rows, _ = recv_ref.shape
    rows = rows // 2
    for shard in range(shards):
        where = slice(shard * rows, (shard + 1) * rows)
        first = 0.5 * (src_ref[where, :] - eps * recv_ref[shard, 0:rows, :])
        first_ref[where, :] = first
        new_ref[where, :] = 0.5 * (first - eps * recv_ref[shard, rows : 2 * rows, :])
    pairs = Listed(list_ref, left_ref.shape[1] // TILE, right_ref.shape[0] // TILE)
    col_scores(
        weight_ref[...], first_ref[...], ln_ref[...], rn_ref[...], right_ref, left_ref, pairs, scr, out_ref
    )
    to_all(send_ref, out_ref[...])


def fine_end(recv_ref, tgt_ref, out_ref):
    out_ref[...] = 0.5 * (tgt_ref[...] - eps * combine(recv_ref[...]))


def scratch_for(left, right, spare):
    rows = left // LANES
    return [
        pltpu.VMEM((rows, LANES), f32),
        pltpu.VMEM((rows, LANES), f32),
        pltpu.VMEM((left // TILE + spare, 8, TILE), f32),
        pltpu.VMEM((8, LANES), f32),
        pltpu.VMEM((right // TILE + spare, TILE, LANES), f32),
        pltpu.VMEM((right, LANES), f32),
        pltpu.VMEM((right, LANES), f32),
    ]


def call(body, outs, operands, scratch=(), smem=(), smem_out=(), work=0):
    spaces = [pltpu.SMEM if i in smem else pltpu.VMEM for i in range(len(operands))]
    out_spaces = [pltpu.SMEM if i in smem_out else pltpu.VMEM for i in range(len(outs))]
    return pl.pallas_call(
        body,
        out_shape=[jax.ShapeDtypeStruct(shape, dtype) for shape, dtype in outs],
        in_specs=[pl.BlockSpec(memory_space=s) for s in spaces],
        out_specs=[pl.BlockSpec(memory_space=s) for s in out_spaces],
        scratch_shapes=list(scratch),
        compiler_params=pltpu.CompilerParams(vmem_limit_bytes=24 * 1024 * 1024),
        cost_estimate=pl.CostEstimate(
            flops=128 * work + 1000, bytes_accessed=1 << 20, transcendentals=work
        ),
    )(*operands)


def exchange(x, axis):
    return lax.all_to_all(x, axis, 0, 0, tiled=True)


def per_device(
    n_src,
    n_tgt,
    src_centroids,
    tgt_centroids,
    src_weights,
    tgt_weights,
    src_cells,
    tgt_cells,
    src_mass,
    tgt_mass,
    src_cluster,
    tgt_cluster,
    support,
    counts,
):
    cs, ct = src_centroids.shape[1], tgt_centroids.shape[1]
    fs, ft = src_cells.shape[1], tgt_cells.shape[1]
    csr, ctr, fsr, ftr = (n // LANES for n in (cs, ct, fs, ft))
    vec = lambda x: x.reshape(-1, LANES)
    src_weights, tgt_weights, src_mass, tgt_mass, src_cluster, tgt_cluster = map(
        vec, (src_weights, tgt_weights, src_mass, tgt_mass, src_cluster, tgt_cluster)
    )
    coarse_scratch = scratch_for(cs, ct, 0)
    fine_scratch = scratch_for(fs, ft, 1)
    one = lambda rows: pltpu.VMEM((rows, LANES), f32)
    coarse_work = cs * ct
    fine_work = fs * ft // 4

    send, right, ln, rn = call(
        coarse_start,
        [((n_src, ctr, LANES), f32), ((ct, LANES), bf16), ((csr, LANES), f32), ((ctr, LANES), f32)],
        [src_centroids, tgt_centroids, src_weights],
        coarse_scratch + [one(ctr)],
        work=coarse_work,
    )
    recv = exchange(send, "src")
    room = support.shape[0] * support.shape[2] + UNROLL
    fine_right, fine_ln, fine_rn, listed = call(
        prepare,
        [
            ((ft, LANES), bf16),
            ((fsr, LANES), f32),
            ((ftr, LANES), f32),
            ((2 * room + 1,), jnp.int32),
        ],
        [src_cells, tgt_cells, support, counts],
        smem=(2, 3),
        smem_out=(3,),
        work=coarse_work,
    )
    send, coarse_tgt = call(
        coarse_rows,
        [((n_tgt, 2 * csr, LANES), f32), ((ctr, LANES), f32)],
        [recv, src_centroids, right, ln, rn, tgt_weights],
        coarse_scratch + [one(csr)],
        work=2 * coarse_work,
    )
    recv = exchange(send, "tgt")
    (send,) = call(
        coarse_cols,
        [((n_src, csr + ctr, LANES), f32)],
        [recv, src_centroids, right, ln, rn, src_weights],
        coarse_scratch + [one(ctr)],
        work=coarse_work,
    )
    every_src = exchange(send, "src")
    (send,) = call(coarse_end, [((n_tgt, ctr, LANES), f32)], [every_src, coarse_tgt])
    every_tgt = exchange(send, "tgt")

    fine_static = [src_cells, fine_right, fine_ln, fine_rn]
    send, fine_src = call(
        fine_cols_first,
        [((n_src, ftr, LANES), f32), ((fsr, LANES), f32)],
        [listed, every_src, src_cluster, *fine_static, src_mass],
        fine_scratch + [one(n_src * csr), one(ftr)],
        smem=(0,),
        work=fine_work,
    )
    recv = exchange(send, "src")
    first_rows, fine_tgt = call(
        fine_rows_first,
        [((fsr, LANES), f32), ((ftr, LANES), f32)],
        [listed, every_tgt, tgt_cluster, *fine_static, tgt_mass],
        fine_scratch + [one(n_tgt * ctr)],
        smem=(0,),
        work=fine_work,
    )
    send, fine_tgt = call(
        fine_rows_second,
        [((n_tgt, 2 * fsr // n_tgt, LANES), f32), ((ftr, LANES), f32)],
        [listed, recv, fine_tgt, first_rows, *fine_static, tgt_mass],
        fine_scratch + [one(fsr)],
        smem=(0,),
        work=fine_work,
    )
    recv = exchange(send, "tgt")
    (send,) = call(combine_rows, [(recv.shape, f32)], [recv])
    recv = exchange(send, "tgt")
    send, fine_src = call(
        fine_cols_second,
        [((n_src, ftr, LANES), f32), ((fsr, LANES), f32)],
        [listed, recv, fine_src, *fine_static, src_mass],
        fine_scratch + [one(fsr), one(ftr)],
        smem=(0,),
        work=fine_work,
    )
    recv = exchange(send, "src")
    (fine_tgt,) = call(fine_end, [((ftr, LANES), f32)], [recv, fine_tgt])
    return (fine_src.reshape(fs), fine_tgt.reshape(ft))


def solution(mesh):
    in_specs = (
        P(None, "src"),
        P(None, "tgt"),
        P("src"),
        P("tgt"),
        P(None, "src"),
        P(None, "tgt"),
        P("src"),
        P("tgt"),
        P("src"),
        P("tgt"),
        P("src", "tgt", None),
        P("src", "tgt"),
    )
    out_specs = (P("src"), P("tgt"))
    body = functools.partial(per_device, mesh.shape["src"], mesh.shape["tgt"])
    return jax.shard_map(body, mesh=mesh, in_specs=in_specs, out_specs=out_specs, check_vma=False)
```

time: 1270 us -> 238 us (0.19)
  the two profiles are of different devices: /device:TPU:32 before, /device:TPU:3 now
where the time goes in v1:
time: 238 us
  blocking collectives  115 us (48%)
  Pallas kernels  85.6 us (36%)
  starting transfers between devices  32.1 us (13%)
  local copies, waits for them, and re-layouts  3.88 us (2%)
    all_to_all x6, blocking collectives, exchange(): return lax.all_to_all(x, axis, 0, 0, tiled=True)  115 us
    pallas_call x11, Pallas kernels, call(): pl.pallas_call(body, out_shape=[jax.ShapeDtypeStruct(shape, dtype) for sh...  85.6 us
    all_to_all x2, starting transfers between devices, exchange(): return lax.all_to_all(x, axis, 0, 0, tiled=True)  32.1 us
  transfers between devices with their start and end apart: 2, of which 0 were waited for; matrix products, arithmetic and copies ran while one was open for 0% of the time, Pallas kernels for 14%

profile of v1, /device:TPU:3, one launch (start us, length us, event | category | flops | bytes accessed | tf_op | source)
XLA Modules:
  0.0 237.5 jit_solution(7520586559877551241)
XLA Ops:
  0.6 0.0 copy-start.2
  0.6 0.9 copy-done.2
  1.5 0.0 copy-start.3
  1.5 0.8 copy-done.3
  2.4 0.0 copy-start.8
  2.4 0.7 copy-done.8
  3.1 0.8 shard_map.132
  3.8 15.0 %all_to_all.40.recv_ref = f32[16,4,128]{2,1,0:T(4,128)S(1)} all-to-all(f32[16,4,128]{2,1,0:T(4,128)S(1)} %get-tuple-element.21), channel_id=1, replica_groups=mesh['src'=16,'tgt'=32] {'src'}, dimensions={0} | all-to-all | bytes 65536 | tf_op jit(solution)/shard_map/all_to_all | solution.py:436
  18.8 0.0 copy-start.10
  18.8 0.7 copy-done.10
  19.5 0.0 copy-start.9
  19.5 1.4 shard_map.133
  20.9 0.0 copy-start
  20.9 24.3 %all_to_all.41.recv_ref = f32[32,16,128]{2,1,0:T(8,128)S(1)} all-to-all(f32[32,16,128]{2,1,0:T(8,128)S(1)} %get-tuple-element.25), channel_id=1, replica_groups=mesh['src'=16,'tgt'=32] {'tgt'}, dimensions={0} | all-to-all | bytes 524288 | tf_op jit(solution)/shard_map/all_to_all | solution.py:436
  45.1 0.0 copy-done.9
  45.1 2.4 %shard_map.134 = f32[16,12,128]{2,1,0:T(8,128)S(1)} custom-call(f32[32,16,128]{2,1,0:T(8,128)S(1)} %all_to_all.41.recv_ref, bf16[64,1024]{1,0:T(8,128)(2,1)S(1)} %copy-done.2, bf16[512,128]{1,0:T(8,128)(2,1)S(1)} %get-tuple-element.22.right_ref, f32[8,128]{1,0:T(8,128)S(1)} %get-tuple-element.23.ln_ref, f32[4,128]{1,0:T(4,128)S(1)} %get-tuple-element.24.rn_ref, ...), custom_call_target="tpu_custom_call" | custom-call | flops 67109864 | bytes 1048576 | tf_op jit(solution)/shard_map/pallas_call | solution.py:422
  47.6 0.0 copy-start.1
  47.6 15.3 %all_to_all.42.recv_ref = f32[16,12,128]{2,1,0:T(8,128)S(1)} all-to-all(f32[16,12,128]{2,1,0:T(8,128)S(1)} %shard_map.134), channel_id=1, replica_groups=mesh['src'=16,'tgt'=32] {'src'}, dimensions={0} | all-to-all | bytes 196608 | tf_op jit(solution)/shard_map/all_to_all | solution.py:436
  62.9 0.7 shard_map.136
  63.6 0.0 copy-start.11
  63.6 5.2 %all-to-all-start.4 = ((f32[32,4,128]{2,1,0:T(4,128)}), f32[32,4,128]{2,1,0:T(4,128)S(1)}, u32[]{:S(2)}, u32[]{:S(2)}) async-start(f32[32,4,128]{2,1,0:T(4,128)} %shard_map.136), calls=%async_computation.4 | async-start | bytes 131072 | tf_op jit(solution)/shard_map/all_to_all | solution.py:436
  68.7 0.0 copy-done.11
  68.7 0.0 copy-start.12
  68.8 0.1 copy.14.support_ref
  68.8 0.6 copy-done.12
  69.4 0.1 copy.15.counts_ref
  69.5 0.0 copy-done
  69.5 0.0 copy-done.1
  69.5 0.0 copy-start.4
  69.5 0.0 copy-start.5
  69.5 2.3 shard_map.131
  71.8 0.0 copy-done.4
  71.8 0.0 copy-done.5
  71.8 9.1 %shard_map.135 = (f32[16,16,128]{2,1,0:T(8,128)}, f32[64,128]{1,0:T(8,128)S(1)}) custom-call(s32[265]{0:T(512)S(1)} %get-tuple-element.20.list_ref, f32[16,12,128]{2,1,0:T(8,128)S(1)} %all_to_all.42.recv_ref, s32[64,128]{1,0:T(8,128)S(1)} %bitcast.8, bf16[64,8192]{1,0:T(8,128)(2,1)S(1)} %copy-done, bf16[2048,128]{1,0:T(8,128)(2,1)S(1)} %get-tuple-element.26.right_ref, ...), custom_call_target="tpu_custom_call" | custom-call | flops 536871936 | bytes 1048576 | tf_op jit(solution)/shard_map/pallas_call | solution.py:422
  80.9 0.0 all-to-all-done.4.recv_ref
  80.9 0.0 copy-start.6
  80.9 0.0 copy-start.7
  80.9 27.0 %all-to-all-start.3 = ((f32[16,16,128]{2,1,0:T(8,128)}), f32[16,16,128]{2,1,0:T(8,128)S(1)}, u32[]{:S(2)}, u32[]{:S(2)}) async-start(f32[16,16,128]{2,1,0:T(8,128)} %get-tuple-element.29), calls=%async_computation.3 | async-start | bytes 262144 | tf_op jit(solution)/shard_map/all_to_all | solution.py:436
  107.9 0.0 copy-done.6
  107.9 0.0 copy-done.7
  107.9 22.7 %shard_map.137 = (f32[64,128]{1,0:T(8,128)S(1)}, f32[16,128]{1,0:T(8,128)S(1)}) custom-call(s32[265]{0:T(512)S(1)} %get-tuple-element.20.list_ref, f32[32,4,128]{2,1,0:T(4,128)S(1)} %all-to-all-done.4.recv_ref, s32[16,128]{1,0:T(8,128)S(1)} %bitcast.11, bf16[64,8192]{1,0:T(8,128)(2,1)S(1)} %copy-done, bf16[2048,128]{1,0:T(8,128)(2,1)S(1)} %get-tuple-element.26.right_ref, ...), custom_call_target="tpu_custom_call" | custom-call | flops 536871936 | bytes 1048576 | tf_op jit(solution)/shard_map/pallas_call | solution.py:422
  130.5 0.0 all-to-all-done.3.recv_ref
  130.6 22.1 %shard_map.138 = (f32[32,4,128]{2,1,0:T(4,128)S(1)}, f32[16,128]{1,0:T(8,128)S(1)}) custom-call(s32[265]{0:T(512)S(1)} %get-tuple-element.20.list_ref, f32[16,16,128]{2,1,0:T(8,128)S(1)} %all-to-all-done.3.recv_ref, f32[16,128]{1,0:T(8,128)S(1)} %get-tuple-element.31.tgt_ref, f32[64,128]{1,0:T(8,128)S(1)} %get-tuple-element.32.first_ref, ...), custom_call_target="tpu_custom_call" | custom-call | flops 536871936 | bytes 1048576 | tf_op jit(solution)/shard_map/pallas_call | solution.py:422
  152.7 18.9 %all_to_all.43.recv_ref = f32[32,4,128]{2,1,0:T(4,128)S(1)} all-to-all(f32[32,4,128]{2,1,0:T(4,128)S(1)} %get-tuple-element.33), channel_id=1, replica_groups=mesh['src'=16,'tgt'=32] {'tgt'}, dimensions={0} | all-to-all | bytes 131072 | tf_op jit(solution)/shard_map/all_to_all | solution.py:436
  171.5 0.1 shard_map.139
  171.6 11.8 %all_to_all.44.recv_ref = f32[32,4,128]{2,1,0:T(4,128)S(1)} all-to-all(f32[32,4,128]{2,1,0:T(4,128)S(1)} %shard_map.139), channel_id=1, replica_groups=mesh['src'=16,'tgt'=32] {'tgt'}, dimensions={0} | all-to-all | bytes 131072 | tf_op jit(solution)/shard_map/all_to_all | solution.py:436
  183.4 23.6 %shard_map.140 = (f32[16,16,128]{2,1,0:T(8,128)S(1)}, f32[64,128]{1,0:T(8,128)}) custom-call(s32[265]{0:T(512)S(1)} %get-tuple-element.20.list_ref, f32[32,4,128]{2,1,0:T(4,128)S(1)} %all_to_all.44.recv_ref, f32[64,128]{1,0:T(8,128)S(1)} %get-tuple-element.34.src_ref, bf16[64,8192]{1,0:T(8,128)(2,1)S(1)} %copy-done, ...), custom_call_target="tpu_custom_call" | custom-call | flops 536871936 | bytes 1048576 | tf_op jit(solution)/shard_map/pallas_call | solution.py:422
  207.0 29.9 %all_to_all.45.recv_ref = f32[16,16,128]{2,1,0:T(8,128)S(1)} all-to-all(f32[16,16,128]{2,1,0:T(8,128)S(1)} %get-tuple-element.36), channel_id=1, replica_groups=mesh['src'=16,'tgt'=32] {'src'}, dimensions={0} | all-to-all | bytes 262144 | tf_op jit(solution)/shard_map/all_to_all | solution.py:436
  236.9 0.6 shard_map.141
Async XLA Ops:
  0.6 0.9 copy-start.2
  1.5 0.8 copy-start.3
  2.4 0.7 copy-start.8
  18.8 0.7 copy-start.10
  19.5 25.6 %copy-start.9 = (f32[1024]{0:T(1024)S(1)}, f32[1024]{0:T(1024)}, u32[]{:S(2)}) copy-start(f32[1024]{0:T(1024)} %param.14) | copy-start | bytes 12292
  20.9 48.6 %copy-start = (bf16[64,8192]{1,0:T(8,128)(2,1)S(1)}, bf16[64,8192]{1,0:T(8,128)(2,1)}, u32[]{:S(2)}) copy-start(bf16[64,8192]{1,0:T(8,128)(2,1)} %left_ref.15) | copy-start | bytes 3145732
  47.6 21.9 %copy-start.1 = (bf16[64,2048]{1,0:T(8,128)(2,1)S(1)}, bf16[64,2048]{1,0:T(8,128)(2,1)}, u32[]{:S(2)}) copy-start(bf16[64,2048]{1,0:T(8,128)(2,1)} %points_ref.2) | copy-start | bytes 786436
  63.6 5.2 %copy-start.11 = (s32[32,1,4]{0,2,1:T(4,128)S(1)}, s32[32,1,4]{0,2,1:T(4,128)}, u32[]{:S(2)}) copy-start(s32[32,1,4]{0,2,1:T(4,128)} %param.22) | copy-start | bytes 1540
  63.6 17.3 %all-to-all-start.4 = ((f32[32,4,128]{2,1,0:T(4,128)}), f32[32,4,128]{2,1,0:T(4,128)S(1)}, u32[]{:S(2)}, u32[]{:S(2)}) async-start(f32[32,4,128]{2,1,0:T(4,128)} %shard_map.136), calls=%async_computation.4 | async-start | bytes 131072 | tf_op jit(solution)/shard_map/all_to_all | solution.py:436
  68.7 0.7 copy-start.12
  69.5 2.3 copy-start.4
  69.5 2.3 copy-start.5
  80.9 27.0 %copy-start.6 = (s32[2048]{0:T(1024)S(1)}, s32[2048]{0:T(1024)}, u32[]{:S(2)}) copy-start(s32[2048]{0:T(1024)} %param.21) | copy-start | bytes 24580
  80.9 27.0 %copy-start.7 = (f32[2048]{0:T(1024)S(1)}, f32[2048]{0:T(1024)}, u32[]{:S(2)}) copy-start(f32[2048]{0:T(1024)} %param.19) | copy-start | bytes 24580
  80.9 49.7 %all-to-all-start.3 = ((f32[16,16,128]{2,1,0:T(8,128)}), f32[16,16,128]{2,1,0:T(8,128)S(1)}, u32[]{:S(2)}, u32[]{:S(2)}) async-start(f32[16,16,128]{2,1,0:T(8,128)} %get-tuple-element.29), calls=%async_computation.3 | async-start | bytes 262144 | tf_op jit(solution)/shard_map/all_to_all | solution.py:436

commit v2 on v1

--- a/solution.py
+++ b/solution.py
@@ -10,7 +10,7 @@
 TILE = 256
 LANES = 128
 HALVES = TILE // LANES
-UNROLL = 4
+UNROLL = 16
 
 eps = 0.0625
 log2e = math.log2(math.e)
@@ -41,6 +41,12 @@
     for row in range(rows.shape[0]):
         spread = jnp.broadcast_to(rows[row : row + 1, :], (LANES, LANES))
         out_ref[row * LANES : (row + 1) * LANES, :] = spread.T
+
+
+def prepare_points(left_ref, points_ref, right_ref, ln_ref, rn_ref):
+    norms_of(left_ref, ln_ref)
+    norms_of(points_ref, rn_ref)
+    transpose_points(points_ref, right_ref)
 
 
 def combine(parts):
@@ -243,15 +249,17 @@
     rest = table - high.astype(f32)
     middle = rest.astype(bf16)
     low = (rest - middle.astype(f32)).astype(bf16)
-    stack = jnp.concatenate([high, middle, low], axis=0)
-    place = lax.broadcasted_iota(jnp.int32, (LANES, LANES), 0)
-    for row in range(which.shape[0]):
-        index = which[row : row + 1, :]
+    upper = jnp.concatenate([high, middle], axis=1)
+    place = lax.broadcasted_iota(jnp.int32, (LANES, TILE), 0)
+    for row in range(0, which.shape[0], HALVES):
+        index = jnp.concatenate([which[row + h : row + h + 1, :] for h in range(HALVES)], axis=1)
         hot = jnp.where(place == lax.shift_right_logical(index, 7), 1.0, 0.0).astype(bf16)
-        found = jnp.dot(stack, hot, preferred_element_type=f32)
-        value = found[:LANES] + found[LANES : 2 * LANES] + found[2 * LANES :]
+        value = jnp.dot(upper, jnp.concatenate([hot, hot], axis=0), preferred_element_type=f32)
+        value = value + jnp.dot(low, hot, preferred_element_type=f32)
         value = jnp.where(place == jnp.bitwise_and(index, LANES - 1), value, 0.0)
-        out_ref[row : row + 1, :] = jnp.sum(value, axis=0, keepdims=True)
+        value = jnp.sum(value, axis=0, keepdims=True)
+        for h in range(HALVES):
+            out_ref[row + h : row + h + 1, :] = half(value, h)
 
 
 def to_all(out_ref, value, start=0):
@@ -260,11 +268,15 @@
     )
 
 
-def coarse_start(left_ref, points_ref, weight_ref, send_ref, right_ref, ln_ref, rn_ref, *scr):
-    norms_of(left_ref, ln_ref)
-    norms_of(points_ref, rn_ref)
-    transpose_points(points_ref, right_ref)
-    *scr, out_ref = scr
+def coarse_start(src_ref, tgt_ref, from_ref, send_ref, *scr):
+    *scr, out_ref, left_ref, points_ref, weight_ref, right_ref, ln_ref, rn_ref, sems = scr
+    moves = ((src_ref, left_ref), (tgt_ref, points_ref), (from_ref, weight_ref))
+    copies = [pltpu.make_async_copy(a, b, sems.at[i]) for i, (a, b) in enumerate(moves)]
+    for copy in copies:
+        copy.start()
+    for copy in copies:
+        copy.wait()
+    prepare_points(left_ref, points_ref, right_ref, ln_ref, rn_ref)
     pairs = Static(left_ref.shape[1] // TILE, points_ref.shape[1] // TILE)
     weight = weight_ref[...]
     pot = jnp.zeros(weight.shape, f32)
@@ -284,7 +296,9 @@
         to_all(send_ref, out_ref[...], step * out_ref.shape[0])
 
 
-def coarse_cols(recv_ref, left_ref, right_ref, ln_ref, rn_ref, weight_ref, send_ref, *scr):
+def coarse_cols(
+    recv_ref, left_ref, right_ref, ln_ref, rn_ref, weight_ref, after_ref, send_ref, *scr
+):
     *scr, out_ref = scr
     lse = combine(recv_ref[...])
     rows = lse.shape[0] // 2
@@ -305,7 +319,9 @@
     to_all(send_ref, 0.5 * (tgt_ref[...] - eps * lse))
 
 
-def prepare(left_ref, points_ref, support_ref, counts_ref, right_ref, ln_ref, rn_ref, list_ref):
+def prepare(
+    left_ref, points_ref, support_ref, counts_ref, after_ref, right_ref, ln_ref, rn_ref, list_ref
+):
     blocks = left_ref.shape[1] // TILE
     tiles = points_ref.shape[1] // TILE
     most = support_ref.shape[2]
@@ -324,9 +340,7 @@
         list_ref[found + u] = blocks
         list_ref[room + found + u] = tiles
     list_ref[2 * room] = lax.div(found + UNROLL - 1, UNROLL)
-    norms_of(left_ref, ln_ref)
-    norms_of(points_ref, rn_ref)
-    transpose_points(points_ref, right_ref)
+    prepare_points(left_ref, points_ref, right_ref, ln_ref, rn_ref)
 
 
 def fine_cols_first(
@@ -416,8 +430,10 @@
     ]
 
 
-def call(body, outs, operands, scratch=(), smem=(), smem_out=(), work=0):
-    spaces = [pltpu.SMEM if i in smem else pltpu.VMEM for i in range(len(operands))]
+def call(body, outs, operands, scratch=(), smem=(), smem_out=(), hbm=(), work=0, limit=24):
+    spaces = [
+        pltpu.SMEM if i in smem else pltpu.HBM if i in hbm else pltpu.VMEM for i in range(len(operands))
+    ]
     out_spaces = [pltpu.SMEM if i in smem_out else pltpu.VMEM for i in range(len(outs))]
     return pl.pallas_call(
         body,
@@ -425,7 +441,7 @@
         in_specs=[pl.BlockSpec(memory_space=s) for s in spaces],
         out_specs=[pl.BlockSpec(memory_space=s) for s in out_spaces],
         scratch_shapes=list(scratch),
-        compiler_params=pltpu.CompilerParams(vmem_limit_bytes=24 * 1024 * 1024),
+        compiler_params=pltpu.CompilerParams(vmem_limit_bytes=limit * 1024 * 1024),
         cost_estimate=pl.CostEstimate(
             flops=128 * work + 1000, bytes_accessed=1 << 20, transcendentals=work
         ),
@@ -465,14 +481,39 @@
     coarse_work = cs * ct
     fine_work = fs * ft // 4
 
-    send, right, ln, rn = call(
+    (send,) = call(
         coarse_start,
-        [((n_src, ctr, LANES), f32), ((ct, LANES), bf16), ((csr, LANES), f32), ((ctr, LANES), f32)],
+        [((n_src, ctr, LANES), f32)],
         [src_centroids, tgt_centroids, src_weights],
-        coarse_scratch + [one(ctr)],
+        coarse_scratch
+        + [
+            one(ctr),
+            pltpu.VMEM(src_centroids.shape, bf16),
+            pltpu.VMEM(tgt_centroids.shape, bf16),
+            one(csr),
+            pltpu.VMEM((ct, LANES), bf16),
+            one(csr),
+            one(ctr),
+            pltpu.SemaphoreType.DMA((3,)),
+        ],
+        hbm=(0, 1, 2),
+        limit=64,
         work=coarse_work,
     )
     recv = exchange(send, "src")
+    right, ln, rn = call(
+        prepare_points,
+        [((ct, LANES), bf16), ((csr, LANES), f32), ((ctr, LANES), f32)],
+        [src_centroids, tgt_centroids],
+        work=coarse_work,
+    )
+    send, coarse_tgt = call(
+        coarse_rows,
+        [((n_tgt, 2 * csr, LANES), f32), ((ctr, LANES), f32)],
+        [recv, src_centroids, right, ln, rn, tgt_weights],
+        coarse_scratch + [one(csr)],
+        work=2 * coarse_work,
+    )
     room = support.shape[0] * support.shape[2] + UNROLL
     fine_right, fine_ln, fine_rn, listed = call(
         prepare,
@@ -482,23 +523,16 @@
             ((ftr, LANES), f32),
             ((2 * room + 1,), jnp.int32),
         ],
-        [src_cells, tgt_cells, support, counts],
+        [src_cells, tgt_cells, support, counts, coarse_tgt],
         smem=(2, 3),
         smem_out=(3,),
-        work=coarse_work,
-    )
-    send, coarse_tgt = call(
-        coarse_rows,
-        [((n_tgt, 2 * csr, LANES), f32), ((ctr, LANES), f32)],
-        [recv, src_centroids, right, ln, rn, tgt_weights],
-        coarse_scratch + [one(csr)],
         work=2 * coarse_work,
     )
     recv = exchange(send, "tgt")
     (send,) = call(
         coarse_cols,
         [((n_src, csr + ctr, LANES), f32)],
-        [recv, src_centroids, right, ln, rn, src_weights],
+        [recv, src_centroids, right, ln, rn, src_weights, fine_rn],
         coarse_scratch + [one(ctr)],
         work=coarse_work,
     )

time: 238 us -> 223 us (0.937)
  the two profiles are of different devices: /device:TPU:3 before, /device:TPU:195 now
where the time goes in v2:
time: 223 us; the launch traced here: 222 us
  blocking collectives  103 us (46%)
  starting transfers between devices  51.7 us (23%)
  Pallas kernels  51 us (23%)
  waiting for transfers between devices  13.5 us (6%)
  local copies, waits for them, and re-layouts  2.35 us (1%)
    all_to_all x4, blocking collectives, exchange(): return lax.all_to_all(x, axis, 0, 0, tiled=True)  103 us
    all_to_all x4, starting transfers between devices, exchange(): return lax.all_to_all(x, axis, 0, 0, tiled=True)  51.7 us
    pallas_call x12, Pallas kernels, call(): pl.pallas_call(body, out_shape=[jax.ShapeDtypeStruct(shape, dtype) for sh...  51 us
    all_to_all x4, waiting for transfers between devices, exchange(): return lax.all_to_all(x, axis, 0, 0, tiled=True)  13.5 us
  transfers between devices with their start and end apart: 4, of which 2 were waited for; matrix products, arithmetic and copies ran while one was open for 0% of the time, Pallas kernels for 14%

profile of v2, /device:TPU:195, one launch (start us, length us, event | category | flops | bytes accessed | tf_op | source)
XLA Modules:
  0.0 222.0 jit_solution(7398487075469996352)
XLA Ops:
  0.6 2.3 %shard_map.131 = f32[16,4,128]{2,1,0:T(4,128)} custom-call(bf16[64,1024]{1,0:T(8,128)(2,1)} %left_ref.11, bf16[64,512]{1,0:T(8,128)(2,1)} %points_ref.2, f32[8,128]{1,0:T(8,128)} %bitcast.14), custom_call_target="tpu_custom_call" | custom-call | flops 67109864 | bytes 1048576 | tf_op jit(solution)/shard_map/pallas_call | solution.py:438
  2.9 0.0 copy-start.4
  3.0 7.9 %all-to-all-start = ((f32[16,4,128]{2,1,0:T(4,128)}), f32[16,4,128]{2,1,0:T(4,128)S(1)}, u32[]{:S(2)}, u32[]{:S(2)}) async-start(f32[16,4,128]{2,1,0:T(4,128)} %shard_map.131), calls=%async_computation | async-start | bytes 65536 | tf_op jit(solution)/shard_map/all_to_all | solution.py:452
  10.9 0.0 copy-done.4
  10.9 0.0 copy-start.2
  10.9 0.9 copy-done.2
  11.8 0.0 copy-start.3
  11.8 0.1 shard_map.132
  11.9 6.4 %all-to-all-done.recv_ref = f32[16,4,128]{2,1,0:T(4,128)S(1)} async-done(((f32[16,4,128]{2,1,0:T(4,128)}), f32[16,4,128]{2,1,0:T(4,128)S(1)}, u32[]{:S(2)}, u32[]{:S(2)}) %all-to-all-start) | async-done | bytes 32800 | tf_op jit(solution)/shard_map/all_to_all | solution.py:452
  18.3 0.0 copy-start.10
  18.3 0.0 copy-done.3
  18.3 0.7 copy-done.10
  19.0 0.0 copy-start
  19.0 3.6 %shard_map.133 = (f32[32,16,128]{2,1,0:T(8,128)}, f32[4,128]{1,0:T(4,128)S(1)}) custom-call(f32[16,4,128]{2,1,0:T(4,128)S(1)} %all-to-all-done.recv_ref, bf16[64,1024]{1,0:T(8,128)(2,1)S(1)} %copy-done.3, bf16[512,128]{1,0:T(8,128)(2,1)S(1)} %get-tuple-element.19.right_ref, f32[8,128]{1,0:T(8,128)S(1)} %get-tuple-element.20.ln_ref, ...), custom_call_target="tpu_custom_call" | custom-call | flops 134218720 | bytes 1048576 | tf_op jit(solution)/shard_map/pallas_call | solution.py:438
  22.5 0.0 copy-start.11
  22.5 0.0 copy-start.1
  22.5 11.8 %all-to-all-start.1 = ((f32[32,16,128]{2,1,0:T(8,128)}), f32[32,16,128]{2,1,0:T(8,128)S(1)}, u32[]{:S(2)}, u32[]{:S(2)}) async-start(f32[32,16,128]{2,1,0:T(8,128)} %get-tuple-element.24), calls=%async_computation.1 | async-start | bytes 524288 | tf_op jit(solution)/shard_map/all_to_all | solution.py:452
  34.4 0.0 copy-done.11
  34.4 0.0 copy-start.12
  34.4 0.1 copy.14.support_ref
  34.5 0.6 copy-done.12
  35.0 0.1 copy.15.counts_ref
  35.1 0.0 copy-done
  35.1 0.0 copy-done.1
  35.1 0.0 copy-start.9
  35.1 2.3 %shard_map.134 = (bf16[2048,128]{1,0:T(8,128)(2,1)S(1)}, f32[64,128]{1,0:T(8,128)S(1)}, f32[16,128]{1,0:T(8,128)S(1)}, s32[289]{0:T(512)S(1)}) custom-call(bf16[64,8192]{1,0:T(8,128)(2,1)S(1)} %copy-done, bf16[64,2048]{1,0:T(8,128)(2,1)S(1)} %copy-done.1, s32[32,1,4]{2,1,0:T(1,128)S(1)} %copy.14.support_ref, s32[32,1]{1,0:T(8,128)S(1)} %copy.15.counts_ref, ...), custom_call_target="tpu_custom_call" | custom-call | flops 134218720 | bytes 1048576 | tf_op jit(solution)/shard_map/pallas_call | solution.py:438
  37.4 7.1 %all-to-all-done.1.recv_ref = f32[32,16,128]{2,1,0:T(8,128)S(1)} async-done(((f32[32,16,128]{2,1,0:T(8,128)}), f32[32,16,128]{2,1,0:T(8,128)S(1)}, u32[]{:S(2)}, u32[]{:S(2)}) %all-to-all-start.1) | async-done | bytes 262176 | tf_op jit(solution)/shard_map/all_to_all | solution.py:452
  44.5 0.0 copy-done.9
  44.5 2.4 %shard_map.135 = f32[16,12,128]{2,1,0:T(8,128)S(1)} custom-call(f32[32,16,128]{2,1,0:T(8,128)S(1)} %all-to-all-done.1.recv_ref, bf16[64,1024]{1,0:T(8,128)(2,1)S(1)} %copy-done.3, bf16[512,128]{1,0:T(8,128)(2,1)S(1)} %get-tuple-element.19.right_ref, f32[8,128]{1,0:T(8,128)S(1)} %get-tuple-element.20.ln_ref, f32[4,128]{1,0:T(4,128)S(1)} %get-tuple-element.21.rn_ref, ...), custom_call_target="tpu_custom_call" | custom-call | flops 67109864 | bytes 1048576 | tf_op jit(solution)/shard_map/pallas_call | solution.py:438
  47.0 12.0 %all_to_all.40.recv_ref = f32[16,12,128]{2,1,0:T(8,128)S(1)} all-to-all(f32[16,12,128]{2,1,0:T(8,128)S(1)} %shard_map.135), channel_id=1, replica_groups=mesh['src'=16,'tgt'=32] {'src'}, dimensions={0} | all-to-all | bytes 196608 | tf_op jit(solution)/shard_map/all_to_all | solution.py:452
  59.0 0.7 shard_map.137
  59.7 0.0 copy-start.5
  59.7 0.0 copy-start.6
  59.7 6.6 %all-to-all-start.4 = ((f32[32,4,128]{2,1,0:T(4,128)}), f32[32,4,128]{2,1,0:T(4,128)S(1)}, u32[]{:S(2)}, u32[]{:S(2)}) async-start(f32[32,4,128]{2,1,0:T(4,128)} %shard_map.137), calls=%async_computation.4 | async-start | bytes 131072 | tf_op jit(solution)/shard_map/all_to_all | solution.py:452
  66.3 0.0 copy-done.5
  66.3 0.0 copy-done.6
  66.3 7.8 %shard_map.136 = (f32[16,16,128]{2,1,0:T(8,128)}, f32[64,128]{1,0:T(8,128)S(1)}) custom-call(s32[289]{0:T(512)S(1)} %get-tuple-element.23.list_ref, f32[16,12,128]{2,1,0:T(8,128)S(1)} %all_to_all.40.recv_ref, s32[64,128]{1,0:T(8,128)S(1)} %bitcast.8, bf16[64,8192]{1,0:T(8,128)(2,1)S(1)} %copy-done, bf16[2048,128]{1,0:T(8,128)(2,1)S(1)} %get-tuple-element.26.right_ref, ...), custom_call_target="tpu_custom_call" | custom-call | flops 536871936 | bytes 1048576 | tf_op jit(solution)/shard_map/pallas_call | solution.py:438
  74.1 0.0 all-to-all-done.4.recv_ref
  74.1 0.0 copy-start.7
  74.1 0.0 copy-start.8
  74.1 25.3 %all-to-all-start.3 = ((f32[16,16,128]{2,1,0:T(8,128)}), f32[16,16,128]{2,1,0:T(8,128)S(1)}, u32[]{:S(2)}, u32[]{:S(2)}) async-start(f32[16,16,128]{2,1,0:T(8,128)} %get-tuple-element.28), calls=%async_computation.3 | async-start | bytes 262144 | tf_op jit(solution)/shard_map/all_to_all | solution.py:452
  99.4 0.0 copy-done.7
  99.4 0.0 copy-done.8
  99.4 20.3 %shard_map.138 = (f32[64,128]{1,0:T(8,128)S(1)}, f32[16,128]{1,0:T(8,128)S(1)}) custom-call(s32[289]{0:T(512)S(1)} %get-tuple-element.23.list_ref, f32[32,4,128]{2,1,0:T(4,128)S(1)} %all-to-all-done.4.recv_ref, s32[16,128]{1,0:T(8,128)S(1)} %bitcast.11, bf16[64,8192]{1,0:T(8,128)(2,1)S(1)} %copy-done, bf16[2048,128]{1,0:T(8,128)(2,1)S(1)} %get-tuple-element.26.right_ref, ...), custom_call_target="tpu_custom_call" | custom-call | flops 536871936 | bytes 1048576 | tf_op jit(solution)/shard_map/pallas_call | solution.py:438
  119.7 0.0 all-to-all-done.3.recv_ref
  119.7 5.1 %shard_map.139 = (f32[32,4,128]{2,1,0:T(4,128)S(1)}, f32[16,128]{1,0:T(8,128)S(1)}) custom-call(s32[289]{0:T(512)S(1)} %get-tuple-element.23.list_ref, f32[16,16,128]{2,1,0:T(8,128)S(1)} %all-to-all-done.3.recv_ref, f32[16,128]{1,0:T(8,128)S(1)} %get-tuple-element.29.tgt_ref, f32[64,128]{1,0:T(8,128)S(1)} %get-tuple-element.30.first_ref, ...), custom_call_target="tpu_custom_call" | custom-call | flops 536871936 | bytes 1048576 | tf_op jit(solution)/shard_map/pallas_call | solution.py:438
  124.8 27.8 %all_to_all.41.recv_ref = f32[32,4,128]{2,1,0:T(4,128)S(1)} all-to-all(f32[32,4,128]{2,1,0:T(4,128)S(1)} %get-tuple-element.31), channel_id=1, replica_groups=mesh['src'=16,'tgt'=32] {'tgt'}, dimensions={0} | all-to-all | bytes 131072 | tf_op jit(solution)/shard_map/all_to_all | solution.py:452
  152.6 0.1 shard_map.140
  152.7 12.0 %all_to_all.42.recv_ref = f32[32,4,128]{2,1,0:T(4,128)S(1)} all-to-all(f32[32,4,128]{2,1,0:T(4,128)S(1)} %shard_map.140), channel_id=1, replica_groups=mesh['src'=16,'tgt'=32] {'tgt'}, dimensions={0} | all-to-all | bytes 131072 | tf_op jit(solution)/shard_map/all_to_all | solution.py:452
  164.7 5.8 %shard_map.141 = (f32[16,16,128]{2,1,0:T(8,128)S(1)}, f32[64,128]{1,0:T(8,128)}) custom-call(s32[289]{0:T(512)S(1)} %get-tuple-element.23.list_ref, f32[32,4,128]{2,1,0:T(4,128)S(1)} %all_to_all.42.recv_ref, f32[64,128]{1,0:T(8,128)S(1)} %get-tuple-element.32.src_ref, bf16[64,8192]{1,0:T(8,128)(2,1)S(1)} %copy-done, ...), custom_call_target="tpu_custom_call" | custom-call | flops 536871936 | bytes 1048576 | tf_op jit(solution)/shard_map/pallas_call | solution.py:438
  170.4 50.9 %all_to_all.43.recv_ref = f32[16,16,128]{2,1,0:T(8,128)S(1)} all-to-all(f32[16,16,128]{2,1,0:T(8,128)S(1)} %get-tuple-element.34), channel_id=1, replica_groups=mesh['src'=16,'tgt'=32] {'src'}, dimensions={0} | all-to-all | bytes 262144 | tf_op jit(solution)/shard_map/all_to_all | solution.py:452
  221.4 0.6 shard_map.142
Async XLA Ops:
  2.9 7.9 %copy-start.4 = (bf16[64,512]{1,0:T(8,128)(2,1)S(1)}, bf16[64,512]{1,0:T(8,128)(2,1)}, u32[]{:S(2)}) copy-start(bf16[64,512]{1,0:T(8,128)(2,1)} %points_ref.2) | copy-start | bytes 196612
  3.0 15.3 %all-to-all-start = ((f32[16,4,128]{2,1,0:T(4,128)}), f32[16,4,128]{2,1,0:T(4,128)S(1)}, u32[]{:S(2)}, u32[]{:S(2)}) async-start(f32[16,4,128]{2,1,0:T(4,128)} %shard_map.131), calls=%async_computation | async-start | bytes 65536 | tf_op jit(solution)/shard_map/all_to_all | solution.py:452
  10.9 0.9 copy-start.2
  11.8 6.5 %copy-start.3 = (bf16[64,1024]{1,0:T(8,128)(2,1)S(1)}, bf16[64,1024]{1,0:T(8,128)(2,1)}, u32[]{:S(2)}) copy-start(bf16[64,1024]{1,0:T(8,128)(2,1)} %left_ref.11) | copy-start | bytes 393220
  18.3 0.7 copy-start.10
  19.0 16.2 %copy-start = (bf16[64,8192]{1,0:T(8,128)(2,1)S(1)}, bf16[64,8192]{1,0:T(8,128)(2,1)}, u32[]{:S(2)}) copy-start(bf16[64,8192]{1,0:T(8,128)(2,1)} %left_ref.15) | copy-start | bytes 3145732
  22.5 11.8 %copy-start.11 = (s32[32,1,4]{0,2,1:T(4,128)S(1)}, s32[32,1,4]{0,2,1:T(4,128)}, u32[]{:S(2)}) copy-start(s32[32,1,4]{0,2,1:T(4,128)} %param.22) | copy-start | bytes 1540
  22.5 12.6 %copy-start.1 = (bf16[64,2048]{1,0:T(8,128)(2,1)S(1)}, bf16[64,2048]{1,0:T(8,128)(2,1)}, u32[]{:S(2)}) copy-start(bf16[64,2048]{1,0:T(8,128)(2,1)} %points_ref.3) | copy-start | bytes 786436
  22.5 22.0 %all-to-all-start.1 = ((f32[32,16,128]{2,1,0:T(8,128)}), f32[32,16,128]{2,1,0:T(8,128)S(1)}, u32[]{:S(2)}, u32[]{:S(2)}) async-start(f32[32,16,128]{2,1,0:T(8,128)} %get-tuple-element.24), calls=%async_computation.1 | async-start | bytes 524288 | tf_op jit(solution)/shard_map/all_to_all | solution.py:452
  34.4 0.7 copy-start.12
  35.1 9.4 %copy-start.9 = (f32[1024]{0:T(1024)S(1)}, f32[1024]{0:T(1024)}, u32[]{:S(2)}) copy-start(f32[1024]{0:T(1024)} %param.14) | copy-start | bytes 12292
  59.7 6.6 %copy-start.5 = (s32[8192]{0:T(1024)S(1)}, s32[8192]{0:T(1024)}, u32[]{:S(2)}) copy-start(s32[8192]{0:T(1024)} %param.20) | copy-start | bytes 98308
  59.7 6.6 %copy-start.6 = (f32[8192]{0:T(1024)S(1)}, f32[8192]{0:T(1024)}, u32[]{:S(2)}) copy-start(f32[8192]{0:T(1024)} %param.18) | copy-start | bytes 98308
  59.7 14.4 %all-to-all-start.4 = ((f32[32,4,128]{2,1,0:T(4,128)}), f32[32,4,128]{2,1,0:T(4,128)S(1)}, u32[]{:S(2)}, u32[]{:S(2)}) async-start(f32[32,4,128]{2,1,0:T(4,128)} %shard_map.137), calls=%async_computation.4 | async-start | bytes 131072 | tf_op jit(solution)/shard_map/all_to_all | solution.py:452
  74.1 25.3 %copy-start.7 = (s32[2048]{0:T(1024)S(1)}, s32[2048]{0:T(1024)}, u32[]{:S(2)}) copy-start(s32[2048]{0:T(1024)} %param.21) | copy-start | bytes 24580
  74.1 25.3 %copy-start.8 = (f32[2048]{0:T(1024)S(1)}, f32[2048]{0:T(1024)}, u32[]{:S(2)}) copy-start(f32[2048]{0:T(1024)} %param.19) | copy-start | bytes 24580
  74.1 45.6 %all-to-all-start.3 = ((f32[16,16,128]{2,1,0:T(8,128)}), f32[16,16,128]{2,1,0:T(8,128)S(1)}, u32[]{:S(2)}, u32[]{:S(2)}) async-start(f32[16,16,128]{2,1,0:T(8,128)} %get-tuple-element.28), calls=%async_computation.3 | async-start | bytes 262144 | tf_op jit(solution)/shard_map/all_to_all | solution.py:452

commit v3 on v2

--- a/solution.py
+++ b/solution.py
@@ -10,7 +10,8 @@
 TILE = 256
 LANES = 128
 HALVES = TILE // LANES
-UNROLL = 16
+UNROLL = 32
+TAIL = 16
 
 eps = 0.0625
 log2e = math.log2(math.e)
@@ -62,7 +63,7 @@
     def __init__(self, blocks, tiles):
         self.blocks, self.tiles = blocks, tiles
 
-    def each(self, step):
+    def each(self, step, unroll=1, tail=1):
         for b in range(self.blocks):
             for k in range(self.tiles):
                 step(b, k, b, k)
@@ -73,16 +74,26 @@
         self.list_ref, self.blocks, self.tiles = list_ref, blocks, tiles
         self.room = (list_ref.shape[0] - 1) // 2
 
-    def each(self, step):
-        def group(index, carry):
-            for u in range(UNROLL):
-                at = index * UNROLL + u
-                b = self.list_ref[at]
-                k = self.list_ref[self.room + at]
-                step(jnp.minimum(b, self.blocks - 1), jnp.minimum(k, self.tiles - 1), b, k)
-            return carry
-
-        lax.fori_loop(0, self.list_ref[2 * self.room], group, 0)
+    def each(self, step, unroll=1, tail=1):
+        def one(pair):
+            b = self.list_ref[pair]
+            k = self.list_ref[self.room + pair]
+            step(jnp.minimum(b, self.blocks - 1), jnp.minimum(k, self.tiles - 1), b, k)
+
+        def groups(first, last, size, start):
+            def group(index, carry):
+                for u in range(size):
+                    one(start + index * size + u)
+                return carry
+
+            lax.fori_loop(first, last, group, 0)
+
+        count = self.list_ref[2 * self.room]
+        whole = lax.div(count, unroll)
+        groups(0, whole, unroll, 0)
+        if unroll > tail:
+            start = whole * unroll
+            groups(0, lax.div(count - start + tail - 1, tail), tail, start)
 
 
 def at(index, size):
@@ -126,15 +137,17 @@
             out_ref[row : row + 1, :] = half(part, h)
 
 
-def col_scores(weight, pot, left_norm, right_norm, right_ref, left_ref, pairs, scr, out_ref):
+def col_scores(
+    weight, pot, left_norm, right_norm, right_ref, left_ref, pairs, scr, out_ref
+):
     dim = left_ref.shape[0]
     scale = 1.0 / (dim * eps)
     vec_ref, vec2_ref, _, _, acc_ref, col_ref, col2_ref = scr
     terms = weight + pot * (1.0 / eps)
     alpha = (terms - left_norm * (0.5 * scale)) * log2e
     top = jnp.max(alpha, keepdims=True)
+    alpha = alpha - top
     rows = alpha.shape[0]
-    vec_ref[0:rows, :] = alpha - top
     acc_ref[...] = jnp.zeros(acc_ref.shape, f32)
 
     def add(b, k, to_b, to_k):
@@ -142,7 +155,8 @@
         parts = [jnp.exp2(half(z, h) + row_of(vec_ref, b, h)) for h in range(HALVES)]
         acc_ref[to_k] += functools.reduce(jnp.add, parts)
 
-    pairs.each(add)
+    vec_ref[0:rows, :] = alpha
+    pairs.each(add, UNROLL, TAIL)
     gather_columns(acc_ref, pairs.tiles, out_ref, jnp.sum)
     total = out_ref[...]
     out_ref[...] = jnp.log(total) + top * ln2 - right_norm * (0.5 * scale)
@@ -180,14 +194,16 @@
         out_ref[...] = peak + jnp.log(out_ref[...])
 
 
-def row_scores(weight, pot, right_norm, left_norm, right_ref, left_ref, pairs, scr, out_ref):
+def row_scores(
+    weight, pot, right_norm, left_norm, right_ref, left_ref, pairs, scr, out_ref
+):
     dim = left_ref.shape[0]
     scale = 1.0 / (dim * eps)
     vec_ref, vec2_ref, acc_ref, _, _, col_ref, col2_ref = scr
     terms = weight + pot * (1.0 / eps)
     beta = (terms - right_norm * (0.5 * scale)) * log2e
     top = jnp.max(beta, keepdims=True)
-    to_columns(beta - top, col_ref)
+    beta = beta - top
     acc_ref[...] = jnp.zeros(acc_ref.shape, f32)
 
     def add(b, k, to_b, to_k):
@@ -197,7 +213,8 @@
             part = by_eights(jnp.exp2(half(z, h) + tgt), jnp.sum)
             acc_ref[to_b, :, h * LANES : (h + 1) * LANES] += part
 
-    pairs.each(add)
+    to_columns(beta, col_ref)
+    pairs.each(add, UNROLL, TAIL)
     gather_rows(acc_ref, pairs.blocks, out_ref, jnp.sum)
     total = out_ref[...]
     out_ref[...] = jnp.log(total) + top * ln2 - left_norm * (0.5 * scale)
@@ -284,16 +301,30 @@
     to_all(send_ref, out_ref[...])
 
 
-def coarse_rows(recv_ref, left_ref, right_ref, ln_ref, rn_ref, weight_ref, send_ref, tgt_ref, *scr):
+def coarse_rows_first(
+    left_ref, points_ref, from_ref, right_ref, ln_ref, rn_ref, weight_ref, out_ref, *scr
+):
+    prepare_points(left_ref, points_ref, right_ref, ln_ref, rn_ref)
+    weight = from_ref[...]
+    weight_ref[...] = weight
+    pairs = Static(left_ref.shape[1] // TILE, right_ref.shape[0] // TILE)
+    pot = jnp.zeros(weight.shape, f32)
+    row_scores(weight, pot, rn_ref[...], ln_ref[...], right_ref, left_ref, pairs, scr, out_ref)
+
+
+def coarse_rows_second(
+    recv_ref, first_ref, left_ref, right_ref, ln_ref, rn_ref, weight_ref, send_ref, tgt_ref, *scr
+):
     *scr, out_ref = scr
     tgt = (-0.5 * eps) * combine(recv_ref[...])
     tgt_ref[...] = tgt
     pairs = Static(left_ref.shape[1] // TILE, right_ref.shape[0] // TILE)
-    for step, pot in enumerate((jnp.zeros(tgt.shape, f32), tgt)):
-        row_scores(
-            weight_ref[...], pot, rn_ref[...], ln_ref[...], right_ref, left_ref, pairs, scr, out_ref
-        )
-        to_all(send_ref, out_ref[...], step * out_ref.shape[0])
+    row_scores(
+        weight_ref[...], tgt, rn_ref[...], ln_ref[...], right_ref, left_ref, pairs, scr, out_ref
+    )
+    first = first_ref[...]
+    to_all(send_ref, first)
+    to_all(send_ref, out_ref[...], first.shape[0])
 
 
 def coarse_cols(
@@ -336,10 +367,10 @@
         return found
 
     found = lax.fori_loop(0, blocks, one_block, 0)
-    for u in range(UNROLL):
+    for u in range(TAIL):
         list_ref[found + u] = blocks
         list_ref[room + found + u] = tiles
-    list_ref[2 * room] = lax.div(found + UNROLL - 1, UNROLL)
+    list_ref[2 * room] = found
     prepare_points(left_ref, points_ref, right_ref, ln_ref, rn_ref)
 
 
@@ -396,16 +427,14 @@
 
 
 def fine_cols_second(
-    list_ref, recv_ref, src_ref, left_ref, right_ref, ln_ref, rn_ref, weight_ref, send_ref, new_ref, *scr
+    list_ref, recv_ref, src_ref, left_ref, right_ref, ln_ref, rn_ref, weight_ref, send_ref, *scr
 ):
     *scr, first_ref, out_ref = scr
     shards, rows, _ = recv_ref.shape
     rows = rows // 2
     for shard in range(shards):
         where = slice(shard * rows, (shard + 1) * rows)
-        first = 0.5 * (src_ref[where, :] - eps * recv_ref[shard, 0:rows, :])
-        first_ref[where, :] = first
-        new_ref[where, :] = 0.5 * (first - eps * recv_ref[shard, rows : 2 * rows, :])
+        first_ref[where, :] = 0.5 * (src_ref[where, :] - eps * recv_ref[shard, 0:rows, :])
     pairs = Listed(list_ref, left_ref.shape[1] // TILE, right_ref.shape[0] // TILE)
     col_scores(
         weight_ref[...], first_ref[...], ln_ref[...], rn_ref[...], right_ref, left_ref, pairs, scr, out_ref
@@ -413,8 +442,14 @@
     to_all(send_ref, out_ref[...])
 
 
-def fine_end(recv_ref, tgt_ref, out_ref):
-    out_ref[...] = 0.5 * (tgt_ref[...] - eps * combine(recv_ref[...]))
+def fine_end(rows_ref, src_ref, recv_ref, tgt_ref, src_out_ref, tgt_out_ref):
+    shards, rows, _ = rows_ref.shape
+    rows = rows // 2
+    for shard in range(shards):
+        where = slice(shard * rows, (shard + 1) * rows)
+        first = 0.5 * (src_ref[where, :] - eps * rows_ref[shard, 0:rows, :])
+        src_out_ref[where, :] = 0.5 * (first - eps * rows_ref[shard, rows : 2 * rows, :])
+    tgt_out_ref[...] = 0.5 * (tgt_ref[...] - eps * combine(recv_ref[...]))
 
 
 def scratch_for(left, right, spare):
@@ -501,20 +536,27 @@
         work=coarse_work,
     )
     recv = exchange(send, "src")
-    right, ln, rn = call(
-        prepare_points,
-        [((ct, LANES), bf16), ((csr, LANES), f32), ((ctr, LANES), f32)],
-        [src_centroids, tgt_centroids],
+    right, ln, rn, tgt_weights, first_rows = call(
+        coarse_rows_first,
+        [
+            ((ct, LANES), bf16),
+            ((csr, LANES), f32),
+            ((ctr, LANES), f32),
+            ((ctr, LANES), f32),
+            ((csr, LANES), f32),
+        ],
+        [src_centroids, tgt_centroids, tgt_weights],
+        coarse_scratch,
         work=coarse_work,
     )
     send, coarse_tgt = call(
-        coarse_rows,
+        coarse_rows_second,
         [((n_tgt, 2 * csr, LANES), f32), ((ctr, LANES), f32)],
-        [recv, src_centroids, right, ln, rn, tgt_weights],
+        [recv, first_rows, src_centroids, right, ln, rn, tgt_weights],
         coarse_scratch + [one(csr)],
-        work=2 * coarse_work,
-    )
-    room = support.shape[0] * support.shape[2] + UNROLL
+        work=coarse_work,
+    )
+    room = support.shape[0] * support.shape[2] + TAIL
     fine_right, fine_ln, fine_rn, listed = call(
         prepare,
         [
@@ -568,17 +610,21 @@
     )
     recv = exchange(send, "tgt")
     (send,) = call(combine_rows, [(recv.shape, f32)], [recv])
-    recv = exchange(send, "tgt")
-    send, fine_src = call(
+    rows = exchange(send, "tgt")
+    (send,) = call(
         fine_cols_second,
-        [((n_src, ftr, LANES), f32), ((fsr, LANES), f32)],
-        [listed, recv, fine_src, *fine_static, src_mass],
+        [((n_src, ftr, LANES), f32)],
+        [listed, rows, fine_src, *fine_static, src_mass],
         fine_scratch + [one(fsr), one(ftr)],
         smem=(0,),
         work=fine_work,
     )
     recv = exchange(send, "src")
-    (fine_tgt,) = call(fine_end, [((ftr, LANES), f32)], [recv, fine_tgt])
+    fine_src, fine_tgt = call(
+        fine_end,
+        [((fsr, LANES), f32), ((ftr, LANES), f32)],
+        [rows, fine_src, recv, fine_tgt],
+    )
     return (fine_src.reshape(fs), fine_tgt.reshape(ft))
 
 

time: 223 us -> 294 us (1.32)
  blocking collectives: 103 us -> 139 us
  Pallas kernels: 51 us -> 74.5 us
  starting transfers between devices: 51.7 us -> 64.6 us
    all_to_all x4, blocking collectives: 103 us -> 139 us  [exchange(): return lax.all_to_all(x, axis, 0, 0, tiled=True)]
    pallas_call x12, Pallas kernels: 51 us -> 74.5 us  [call(): pl.pallas_call(body, out_shape=[jax.ShapeDtypeStruct(shape, dtype) for sh...]
    all_to_all x4, starting transfers between devices: 51.7 us -> 64.6 us  [exchange(): return lax.all_to_all(x, axis, 0, 0, tiled=True)]
  transfers between devices with their start and end apart: 4 -> 4, of which waited for: 2 -> 2; matrix products, arithmetic and copies ran while one was open for 0% -> 0% of each run, Pallas kernels for 14% -> 10%
where the time goes in v3:
time: 294 us; the launch traced here: 293 us
  blocking collectives  139 us (47%)
  Pallas kernels  74.5 us (25%)
  starting transfers between devices  64.6 us (22%)
  waiting for transfers between devices  10.8 us (4%)
  local copies, waits for them, and re-layouts  3.26 us (1%)
    all_to_all x4, blocking collectives, exchange(): return lax.all_to_all(x, axis, 0, 0, tiled=True)  139 us
    pallas_call x12, Pallas kernels, call(): pl.pallas_call(body, out_shape=[jax.ShapeDtypeStruct(shape, dtype) for sh...  74.5 us
    all_to_all x4, starting transfers between devices, exchange(): return lax.all_to_all(x, axis, 0, 0, tiled=True)  64.6 us
    all_to_all x4, waiting for transfers between devices, exchange(): return lax.all_to_all(x, axis, 0, 0, tiled=True)  10.8 us
  transfers between devices with their start and end apart: 4, of which 2 were waited for; matrix products, arithmetic and copies ran while one was open for 0% of the time, Pallas kernels for 10%

profile of v3, /device:TPU:195, one launch (start us, length us, event | category | flops | bytes accessed | tf_op | source)
XLA Modules:
  0.0 293.1 jit_solution(11634760017450252629)
XLA Ops:
  0.6 2.3 shard_map.131
  2.9 0.0 copy-start.5
  3.0 7.9 %all-to-all-start = ((f32[16,4,128]{2,1,0:T(4,128)}), f32[16,4,128]{2,1,0:T(4,128)S(1)}, u32[]{:S(2)}, u32[]{:S(2)}) async-start(f32[16,4,128]{2,1,0:T(4,128)} %shard_map.131), calls=%async_computation | async-start | bytes 65536 | tf_op jit(solution)/shard_map/all_to_all | solution.py:487
  10.9 0.0 copy-done.5
  10.9 0.0 copy-start.2
  10.9 0.9 copy-done.2
  11.8 0.0 copy-start.11
  11.8 0.7 copy-done.11
  12.5 0.0 copy-start
  12.5 0.7 shard_map.132
  13.2 5.1 %all-to-all-done.recv_ref = f32[16,4,128]{2,1,0:T(4,128)S(1)} async-done(((f32[16,4,128]{2,1,0:T(4,128)}), f32[16,4,128]{2,1,0:T(4,128)S(1)}, u32[]{:S(2)}, u32[]{:S(2)}) %all-to-all-start) | async-done | bytes 32800 | tf_op jit(solution)/shard_map/all_to_all | solution.py:487
  18.3 0.0 copy-start.3
  18.3 0.9 copy-done.3
  19.2 1.4 shard_map.133
  20.6 0.0 copy-start.12
  20.6 0.0 copy-start.1
  20.6 13.4 %all-to-all-start.1 = ((f32[32,16,128]{2,1,0:T(8,128)}), f32[32,16,128]{2,1,0:T(8,128)S(1)}, u32[]{:S(2)}, u32[]{:S(2)}) async-start(f32[32,16,128]{2,1,0:T(8,128)} %get-tuple-element.28), calls=%async_computation.1 | async-start | bytes 524288 | tf_op jit(solution)/shard_map/all_to_all | solution.py:487
  34.1 0.0 copy-done.12
  34.1 0.0 copy-start.13
  34.1 0.1 copy.14.support_ref
  34.2 0.6 copy-done.13
  34.7 0.1 copy.15.counts_ref
  34.8 0.0 copy-done
  34.8 0.0 copy-done.1
  34.8 0.0 copy-start.4
  34.8 0.0 copy-start.10
  34.9 2.3 shard_map.134
  37.1 5.8 %all-to-all-done.1.recv_ref = f32[32,16,128]{2,1,0:T(8,128)S(1)} async-done(((f32[32,16,128]{2,1,0:T(8,128)}), f32[32,16,128]{2,1,0:T(8,128)S(1)}, u32[]{:S(2)}, u32[]{:S(2)}) %all-to-all-start.1) | async-done | bytes 262176 | tf_op jit(solution)/shard_map/all_to_all | solution.py:487
  42.9 0.0 copy-done.4
  42.9 0.0 copy-done.10
  42.9 2.4 shard_map.135
  45.3 14.0 %all_to_all.40.recv_ref = f32[16,12,128]{2,1,0:T(8,128)S(1)} all-to-all(f32[16,12,128]{2,1,0:T(8,128)S(1)} %shard_map.135), channel_id=1, replica_groups=mesh['src'=16,'tgt'=32] {'src'}, dimensions={0} | all-to-all | bytes 196608 | tf_op jit(solution)/shard_map/all_to_all | solution.py:487
  59.3 0.7 shard_map.137
  60.0 0.0 copy-start.6
  60.0 0.0 copy-start.7
  60.0 6.5 %all-to-all-start.4 = ((f32[32,4,128]{2,1,0:T(4,128)}), f32[32,4,128]{2,1,0:T(4,128)S(1)}, u32[]{:S(2)}, u32[]{:S(2)}) async-start(f32[32,4,128]{2,1,0:T(4,128)} %shard_map.137), calls=%async_computation.4 | async-start | bytes 131072 | tf_op jit(solution)/shard_map/all_to_all | solution.py:487
  66.5 0.0 copy-done.6
  66.5 0.0 copy-done.7
  66.5 6.1 %shard_map.136 = (f32[16,16,128]{2,1,0:T(8,128)}, f32[64,128]{1,0:T(8,128)S(1)}) custom-call(s32[289]{0:T(512)S(1)} %get-tuple-element.27.list_ref, f32[16,12,128]{2,1,0:T(8,128)S(1)} %all_to_all.40.recv_ref, s32[64,128]{1,0:T(8,128)S(1)} %bitcast.8, bf16[64,8192]{1,0:T(8,128)(2,1)S(1)} %copy-done, bf16[2048,128]{1,0:T(8,128)(2,1)S(1)} %get-tuple-element.30.right_ref, ...), custom_call_target="tpu_custom_call" | custom-call | flops 536871936 | bytes 1048576 | tf_op jit(solution)/shard_map/pallas_call | solution.py:473
  72.7 0.0 all-to-all-done.4.recv_ref
  72.7 0.0 copy-start.8
  72.7 0.0 copy-start.9
  72.7 36.7 %all-to-all-start.3 = ((f32[16,16,128]{2,1,0:T(8,128)}), f32[16,16,128]{2,1,0:T(8,128)S(1)}, u32[]{:S(2)}, u32[]{:S(2)}) async-start(f32[16,16,128]{2,1,0:T(8,128)} %get-tuple-element.32), calls=%async_computation.3 | async-start | bytes 262144 | tf_op jit(solution)/shard_map/all_to_all | solution.py:487
  109.4 0.0 copy-done.8
  109.4 0.0 copy-done.9
  109.4 19.3 %shard_map.138 = (f32[64,128]{1,0:T(8,128)S(1)}, f32[16,128]{1,0:T(8,128)S(1)}) custom-call(s32[289]{0:T(512)S(1)} %get-tuple-element.27.list_ref, f32[32,4,128]{2,1,0:T(4,128)S(1)} %all-to-all-done.4.recv_ref, s32[16,128]{1,0:T(8,128)S(1)} %bitcast.11, bf16[64,8192]{1,0:T(8,128)(2,1)S(1)} %copy-done, bf16[2048,128]{1,0:T(8,128)(2,1)S(1)} %get-tuple-element.30.right_ref, ...), custom_call_target="tpu_custom_call" | custom-call | flops 536871936 | bytes 1048576 | tf_op jit(solution)/shard_map/pallas_call | solution.py:473
  128.7 0.0 all-to-all-done.3.recv_ref
  128.7 19.0 %shard_map.139 = (f32[32,4,128]{2,1,0:T(4,128)S(1)}, f32[16,128]{1,0:T(8,128)S(1)}) custom-call(s32[289]{0:T(512)S(1)} %get-tuple-element.27.list_ref, f32[16,16,128]{2,1,0:T(8,128)S(1)} %all-to-all-done.3.recv_ref, f32[16,128]{1,0:T(8,128)S(1)} %get-tuple-element.33.tgt_ref, f32[64,128]{1,0:T(8,128)S(1)} %get-tuple-element.34.first_ref, ...), custom_call_target="tpu_custom_call" | custom-call | flops 536871936 | bytes 1048576 | tf_op jit(solution)/shard_map/pallas_call | solution.py:473
  147.8 51.3 %all_to_all.41.recv_ref = f32[32,4,128]{2,1,0:T(4,128)S(1)} all-to-all(f32[32,4,128]{2,1,0:T(4,128)S(1)} %get-tuple-element.35), channel_id=1, replica_groups=mesh['src'=16,'tgt'=32] {'tgt'}, dimensions={0} | all-to-all | bytes 131072 | tf_op jit(solution)/shard_map/all_to_all | solution.py:487
  199.1 0.1 shard_map.140
  199.2 12.4 %all_to_all.42.recv_ref.rows_ref = f32[32,4,128]{2,1,0:T(4,128)S(1)} all-to-all(f32[32,4,128]{2,1,0:T(4,128)S(1)} %shard_map.140), channel_id=1, replica_groups=mesh['src'=16,'tgt'=32] {'tgt'}, dimensions={0} | all-to-all | bytes 131072 | tf_op jit(solution)/shard_map/all_to_all | solution.py:487
  211.5 19.4 %shard_map.141 = f32[16,16,128]{2,1,0:T(8,128)S(1)} custom-call(s32[289]{0:T(512)S(1)} %get-tuple-element.27.list_ref, f32[32,4,128]{2,1,0:T(4,128)S(1)} %all_to_all.42.recv_ref.rows_ref, f32[64,128]{1,0:T(8,128)S(1)} %get-tuple-element.36.src_ref, bf16[64,8192]{1,0:T(8,128)(2,1)S(1)} %copy-done, bf16[2048,128]{1,0:T(8,128)(2,1)S(1)} %get-tuple-element.30.right_ref, ...), custom_call_target="tpu_custom_call" | custom-call | flops 536871936 | bytes 1048576 | tf_op jit(solution)/shard_map/pallas_call | solution.py:473
  231.0 61.4 %all_to_all.43.recv_ref = f32[16,16,128]{2,1,0:T(8,128)S(1)} all-to-all(f32[16,16,128]{2,1,0:T(8,128)S(1)} %shard_map.141), channel_id=1, replica_groups=mesh['src'=16,'tgt'=32] {'src'}, dimensions={0} | all-to-all | bytes 262144 | tf_op jit(solution)/shard_map/all_to_all | solution.py:487
  292.4 0.7 shard_map.142
Async XLA Ops:
  2.9 7.9 %copy-start.5 = (bf16[64,512]{1,0:T(8,128)(2,1)S(1)}, bf16[64,512]{1,0:T(8,128)(2,1)}, u32[]{:S(2)}) copy-start(bf16[64,512]{1,0:T(8,128)(2,1)} %points_ref.2) | copy-start | bytes 196612
  3.0 15.3 %all-to-all-start = ((f32[16,4,128]{2,1,0:T(4,128)}), f32[16,4,128]{2,1,0:T(4,128)S(1)}, u32[]{:S(2)}, u32[]{:S(2)}) async-start(f32[16,4,128]{2,1,0:T(4,128)} %shard_map.131), calls=%async_computation | async-start | bytes 65536 | tf_op jit(solution)/shard_map/all_to_all | solution.py:487
  10.9 0.9 copy-start.2
  11.8 0.7 copy-start.11
  12.5 22.4 %copy-start = (bf16[64,8192]{1,0:T(8,128)(2,1)S(1)}, bf16[64,8192]{1,0:T(8,128)(2,1)}, u32[]{:S(2)}) copy-start(bf16[64,8192]{1,0:T(8,128)(2,1)} %left_ref.15) | copy-start | bytes 3145732
  18.3 0.9 copy-start.3
  20.6 13.5 %copy-start.12 = (s32[32,1,4]{0,2,1:T(4,128)S(1)}, s32[32,1,4]{0,2,1:T(4,128)}, u32[]{:S(2)}) copy-start(s32[32,1,4]{0,2,1:T(4,128)} %param.22) | copy-start | bytes 1540
  20.6 14.2 %copy-start.1 = (bf16[64,2048]{1,0:T(8,128)(2,1)S(1)}, bf16[64,2048]{1,0:T(8,128)(2,1)}, u32[]{:S(2)}) copy-start(bf16[64,2048]{1,0:T(8,128)(2,1)} %points_ref.3) | copy-start | bytes 786436
  20.6 22.3 %all-to-all-start.1 = ((f32[32,16,128]{2,1,0:T(8,128)}), f32[32,16,128]{2,1,0:T(8,128)S(1)}, u32[]{:S(2)}, u32[]{:S(2)}) async-start(f32[32,16,128]{2,1,0:T(8,128)} %get-tuple-element.28), calls=%async_computation.1 | async-start | bytes 524288 | tf_op jit(solution)/shard_map/all_to_all | solution.py:487
  34.1 0.7 copy-start.13
  34.8 8.1 %copy-start.4 = (bf16[64,1024]{1,0:T(8,128)(2,1)S(1)}, bf16[64,1024]{1,0:T(8,128)(2,1)}, u32[]{:S(2)}) copy-start(bf16[64,1024]{1,0:T(8,128)(2,1)} %left_ref.11) | copy-start | bytes 393220
  34.8 8.1 %copy-start.10 = (f32[1024]{0:T(1024)S(1)}, f32[1024]{0:T(1024)}, u32[]{:S(2)}) copy-start(f32[1024]{0:T(1024)} %param.14) | copy-start | bytes 12292
  60.0 6.5 %copy-start.6 = (s32[8192]{0:T(1024)S(1)}, s32[8192]{0:T(1024)}, u32[]{:S(2)}) copy-start(s32[8192]{0:T(1024)} %param.20) | copy-start | bytes 98308
  60.0 6.5 %copy-start.7 = (f32[8192]{0:T(1024)S(1)}, f32[8192]{0:T(1024)}, u32[]{:S(2)}) copy-start(f32[8192]{0:T(1024)} %param.18) | copy-start | bytes 98308
  60.0 12.7 %all-to-all-start.4 = ((f32[32,4,128]{2,1,0:T(4,128)}), f32[32,4,128]{2,1,0:T(4,128)S(1)}, u32[]{:S(2)}, u32[]{:S(2)}) async-start(f32[32,4,128]{2,1,0:T(4,128)} %shard_map.137), calls=%async_computation.4 | async-start | bytes 131072 | tf_op jit(solution)/shard_map/all_to_all | solution.py:487
  72.7 36.7 %copy-start.8 = (s32[2048]{0:T(1024)S(1)}, s32[2048]{0:T(1024)}, u32[]{:S(2)}) copy-start(s32[2048]{0:T(1024)} %param.21) | copy-start | bytes 24580
  72.7 36.7 %copy-start.9 = (f32[2048]{0:T(1024)S(1)}, f32[2048]{0:T(1024)}, u32[]{:S(2)}) copy-start(f32[2048]{0:T(1024)} %param.19) | copy-start | bytes 24580
  72.7 56.0 %all-to-all-start.3 = ((f32[16,16,128]{2,1,0:T(8,128)}), f32[16,16,128]{2,1,0:T(8,128)S(1)}, u32[]{:S(2)}, u32[]{:S(2)}) async-start(f32[16,16,128]{2,1,0:T(8,128)} %get-tuple-element.32), calls=%async_computation.3 | async-start | bytes 262144 | tf_op jit(solution)/shard_map/all_to_all | solution.py:487

commit v4 on v3

--- a/solution.py
+++ b/solution.py
@@ -12,12 +12,16 @@
 HALVES = TILE // LANES
 UNROLL = 32
 TAIL = 16
+CHUNK = 8
+CHUNKS = 5
+PAIRS_A_CHUNK = 20
 
 eps = 0.0625
 log2e = math.log2(math.e)
 ln2 = math.log(2.0)
 smallest = 1e-25
 largest = 1e37
+farthest = -120.0
 very_low = -3e38
 
 f32 = jnp.float32
@@ -55,45 +59,74 @@
     return peak + jnp.log(jnp.sum(jnp.exp(parts - peak[None]), axis=0))
 
 
-def in_range(total):
-    return jnp.logical_and(jnp.min(total) >= smallest, jnp.max(total) <= largest)
+def in_range(total, own):
+    total_fits = jnp.logical_and(jnp.min(total) >= smallest, jnp.max(total) <= largest)
+    return jnp.logical_and(total_fits, jnp.min(own) >= farthest)
 
 
 class Static:
     def __init__(self, blocks, tiles):
         self.blocks, self.tiles = blocks, tiles
 
-    def each(self, step, unroll=1, tail=1):
+    def each_fast(self, step, step_held):
+        self.each(step)
+
+    def each(self, step):
         for b in range(self.blocks):
             for k in range(self.tiles):
                 step(b, k, b, k)
 
 
 class Listed:
-    def __init__(self, list_ref, blocks, tiles):
+    def __init__(self, list_ref, blocks, tiles, stored_ref=None, held_ref=None, sems=None):
         self.list_ref, self.blocks, self.tiles = list_ref, blocks, tiles
-        self.room = (list_ref.shape[0] - 1) // 2
-
-    def each(self, step, unroll=1, tail=1):
-        def one(pair):
-            b = self.list_ref[pair]
-            k = self.list_ref[self.room + pair]
-            step(jnp.minimum(b, self.blocks - 1), jnp.minimum(k, self.tiles - 1), b, k)
-
-        def groups(first, last, size, start):
+        self.held_ref = held_ref
+        self.room = (list_ref.shape[0] - 2) // 2
+        self.count = list_ref[2 * self.room]
+        self.chunks = list_ref[2 * self.room + 1]
+        self.copies = []
+        if stored_ref is not None:
+            for chunk in range(CHUNKS):
+                where = pl.ds(chunk * CHUNK, CHUNK)
+                self.copies.append(
+                    pltpu.make_async_copy(stored_ref.at[where], held_ref.at[where], sems.at[chunk])
+                )
+                pl.when(chunk < self.chunks)(self.copies[-1].start)
+
+    def of(self, pair):
+        return self.list_ref[pair], self.list_ref[self.room + pair]
+
+    def clip(self, b, k):
+        return jnp.minimum(b, self.blocks - 1), jnp.minimum(k, self.tiles - 1)
+
+    def each(self, step, unroll=1, tail=1, first=0):
+        def groups(number, size, start):
             def group(index, carry):
                 for u in range(size):
-                    one(start + index * size + u)
+                    b, k = self.of(start + index * size + u)
+                    step(*self.clip(b, k), b, k)
                 return carry
 
-            lax.fori_loop(first, last, group, 0)
-
-        count = self.list_ref[2 * self.room]
+            lax.fori_loop(0, number, group, 0)
+
+        count = self.count - first
         whole = lax.div(count, unroll)
-        groups(0, whole, unroll, 0)
+        groups(whole, unroll, first)
         if unroll > tail:
-            start = whole * unroll
-            groups(0, lax.div(count - start + tail - 1, tail), tail, start)
+            done = whole * unroll
+            groups(lax.div(count - done + tail - 1, tail), tail, first + done)
+
+    def each_fast(self, step, step_held):
+        if not self.copies:
+            return self.each(step, UNROLL, TAIL)
+        self.each(step, UNROLL, TAIL, self.chunks * CHUNK)
+        for chunk, copy in enumerate(self.copies):
+
+            @pl.when(chunk < self.chunks)
+            def _():
+                copy.wait()
+                for pair in range(chunk * CHUNK, (chunk + 1) * CHUNK):
+                    step_held(self.held_ref.at[pair], *self.of(pair))
 
 
 def at(index, size):
@@ -156,12 +189,20 @@
         acc_ref[to_k] += functools.reduce(jnp.add, parts)
 
     vec_ref[0:rows, :] = alpha
-    pairs.each(add, UNROLL, TAIL)
+    vec2_ref[0:rows, :] = jnp.exp2(alpha)
+
+    def add_held(e_ref, b, k):
+        parts = [
+            e_ref[:, h * LANES : (h + 1) * LANES] * row_of(vec2_ref, b, h) for h in range(HALVES)
+        ]
+        acc_ref[k] += functools.reduce(jnp.add, parts)
+
+    pairs.each_fast(add, add_held)
     gather_columns(acc_ref, pairs.tiles, out_ref, jnp.sum)
     total = out_ref[...]
     out_ref[...] = jnp.log(total) + top * ln2 - right_norm * (0.5 * scale)
 
-    @pl.when(jnp.logical_not(in_range(total)))
+    @pl.when(jnp.logical_not(in_range(total, alpha)))
     def _():
         vec_ref[0:rows, :] = terms
         vec2_ref[0:rows, :] = left_norm
@@ -214,12 +255,19 @@
             acc_ref[to_b, :, h * LANES : (h + 1) * LANES] += part
 
     to_columns(beta, col_ref)
-    pairs.each(add, UNROLL, TAIL)
+    col2_ref[...] = jnp.exp2(col_ref[...])
+    def add_held(e_ref, b, k):
+        tgt = col2_ref[at(k, TILE), :]
+        for h in range(HALVES):
+            where = slice(h * LANES, (h + 1) * LANES)
+            acc_ref[b, :, where] += by_eights(e_ref[:, where] * tgt, jnp.sum)
+
+    pairs.each_fast(add, add_held)
     gather_rows(acc_ref, pairs.blocks, out_ref, jnp.sum)
     total = out_ref[...]
     out_ref[...] = jnp.log(total) + top * ln2 - left_norm * (0.5 * scale)
 
-    @pl.when(jnp.logical_not(in_range(total)))
+    @pl.when(jnp.logical_not(in_range(total, beta)))
     def _():
         rows = left_norm.shape[0]
         to_columns(terms, col_ref)
@@ -302,8 +350,9 @@
 
 
 def coarse_rows_first(
-    left_ref, points_ref, from_ref, right_ref, ln_ref, rn_ref, weight_ref, out_ref, *scr
-):
+    src_ref, points_ref, from_ref, left_ref, right_ref, ln_ref, rn_ref, weight_ref, out_ref, *scr
+):
+    left_ref[...] = src_ref[...]
     prepare_points(left_ref, points_ref, right_ref, ln_ref, rn_ref)
     weight = from_ref[...]
     weight_ref[...] = weight
@@ -328,9 +377,10 @@
 
 
 def coarse_cols(
-    recv_ref, left_ref, right_ref, ln_ref, rn_ref, weight_ref, after_ref, send_ref, *scr
+    recv_ref, left_ref, right_ref, ln_ref, rn_ref, weight_ref, after_ref, send_ref, done_ref, *scr
 ):
     *scr, out_ref = scr
+    done_ref[...] = jnp.zeros(done_ref.shape, f32)
     lse = combine(recv_ref[...])
     rows = lse.shape[0] // 2
     first = (-0.5 * eps) * lse[:rows]
@@ -343,7 +393,27 @@
     to_all(send_ref, out_ref[...], rows)
 
 
-def coarse_end(recv_ref, tgt_ref, send_ref):
+def store_some(list_ref, left_ref, right_ref, after_ref, stored_ref, done_ref, held_ref, sems):
+    done_ref[...] = after_ref[...]
+    dim = left_ref.shape[0]
+    pairs = Listed(list_ref, left_ref.shape[1] // TILE, right_ref.shape[0] // TILE)
+    for wait in (False, True):
+        for chunk in range(CHUNKS):
+            where = pl.ds(chunk * CHUNK, CHUNK)
+            copy = pltpu.make_async_copy(held_ref.at[where], stored_ref.at[where], sems.at[chunk])
+
+            @pl.when(chunk < pairs.chunks)
+            def _():
+                if wait:
+                    copy.wait()
+                    return
+                for pair in range(chunk * CHUNK, (chunk + 1) * CHUNK):
+                    z = inner_of(right_ref, left_ref, *pairs.of(pair))
+                    held_ref[pair] = jnp.exp2(z * (log2e / (dim * eps)))
+                copy.start()
+
+
+def coarse_end(recv_ref, tgt_ref, after_ref, send_ref):
     count = tgt_ref.shape[0]
     rows = recv_ref.shape[1] - count
     lse = combine(recv_ref[:, rows:, :])
@@ -356,7 +426,7 @@
     blocks = left_ref.shape[1] // TILE
     tiles = points_ref.shape[1] // TILE
     most = support_ref.shape[2]
-    room = (list_ref.shape[0] - 1) // 2
+    room = (list_ref.shape[0] - 2) // 2
 
     def one_block(b, found):
         count = counts_ref[b, 0]
@@ -371,19 +441,22 @@
         list_ref[found + u] = blocks
         list_ref[room + found + u] = tiles
     list_ref[2 * room] = found
+    list_ref[2 * room + 1] = jnp.minimum(lax.div(found, PAIRS_A_CHUNK), CHUNKS)
     prepare_points(left_ref, points_ref, right_ref, ln_ref, rn_ref)
 
 
 def fine_cols_first(
-    list_ref, recv_ref, which_ref, left_ref, right_ref, ln_ref, rn_ref, weight_ref, send_ref, src_ref, *scr
-):
-    *scr, table_ref, out_ref = scr
+    list_ref, stored_ref, recv_ref, which_ref, left_ref, right_ref, ln_ref, rn_ref, weight_ref, send_ref, src_ref, *scr
+):
+    *scr, table_ref, out_ref, held_ref, sems = scr
+    pairs = Listed(
+        list_ref, left_ref.shape[1] // TILE, right_ref.shape[0] // TILE, stored_ref, held_ref, sems
+    )
     shards = recv_ref.shape[0]
     rows = table_ref.shape[0] // shards
     for shard in range(shards):
         table_ref[shard * rows : (shard + 1) * rows, :] = recv_ref[shard, 0:rows, :]
     look_up(table_ref[...], which_ref[...], src_ref)
-    pairs = Listed(list_ref, left_ref.shape[1] // TILE, right_ref.shape[0] // TILE)
     col_scores(
         weight_ref[...], src_ref[...], ln_ref[...], rn_ref[...], right_ref, left_ref, pairs, scr, out_ref
     )
@@ -391,26 +464,30 @@
 
 
 def fine_rows_first(
-    list_ref, recv_ref, which_ref, left_ref, right_ref, ln_ref, rn_ref, weight_ref, out_ref, tgt_ref, *scr
-):
-    *scr, table_ref = scr
+    list_ref, stored_ref, recv_ref, which_ref, left_ref, right_ref, ln_ref, rn_ref, weight_ref, out_ref, tgt_ref, *scr
+):
+    *scr, table_ref, held_ref, sems = scr
+    pairs = Listed(
+        list_ref, left_ref.shape[1] // TILE, right_ref.shape[0] // TILE, stored_ref, held_ref, sems
+    )
     shards = recv_ref.shape[0]
     rows = table_ref.shape[0] // shards
     for shard in range(shards):
         table_ref[shard * rows : (shard + 1) * rows, :] = recv_ref[shard]
     look_up(table_ref[...], which_ref[...], tgt_ref)
-    pairs = Listed(list_ref, left_ref.shape[1] // TILE, right_ref.shape[0] // TILE)
     row_scores(
         weight_ref[...], tgt_ref[...], rn_ref[...], ln_ref[...], right_ref, left_ref, pairs, scr, out_ref
     )
 
 
 def fine_rows_second(
-    list_ref, recv_ref, tgt_ref, first_ref, left_ref, right_ref, ln_ref, rn_ref, weight_ref, send_ref, new_ref, *scr
-):
-    *scr, out_ref = scr
+    list_ref, stored_ref, recv_ref, tgt_ref, first_ref, left_ref, right_ref, ln_ref, rn_ref, weight_ref, send_ref, new_ref, *scr
+):
+    *scr, out_ref, held_ref, sems = scr
+    pairs = Listed(
+        list_ref, left_ref.shape[1] // TILE, right_ref.shape[0] // TILE, stored_ref, held_ref, sems
+    )
     new_ref[...] = 0.5 * (tgt_ref[...] - eps * combine(recv_ref[...]))
-    pairs = Listed(list_ref, left_ref.shape[1] // TILE, right_ref.shape[0] // TILE)
     row_scores(
         weight_ref[...], new_ref[...], rn_ref[...], ln_ref[...], right_ref, left_ref, pairs, scr, out_ref
     )
@@ -427,15 +504,17 @@
 
 
 def fine_cols_second(
-    list_ref, recv_ref, src_ref, left_ref, right_ref, ln_ref, rn_ref, weight_ref, send_ref, *scr
-):
-    *scr, first_ref, out_ref = scr
+    list_ref, stored_ref, recv_ref, src_ref, left_ref, right_ref, ln_ref, rn_ref, weight_ref, send_ref, *scr
+):
+    *scr, first_ref, out_ref, held_ref, sems = scr
+    pairs = Listed(
+        list_ref, left_ref.shape[1] // TILE, right_ref.shape[0] // TILE, stored_ref, held_ref, sems
+    )
     shards, rows, _ = recv_ref.shape
     rows = rows // 2
     for shard in range(shards):
         where = slice(shard * rows, (shard + 1) * rows)
         first_ref[where, :] = 0.5 * (src_ref[where, :] - eps * recv_ref[shard, 0:rows, :])
-    pairs = Listed(list_ref, left_ref.shape[1] // TILE, right_ref.shape[0] // TILE)
     col_scores(
         weight_ref[...], first_ref[...], ln_ref[...], rn_ref[...], right_ref, left_ref, pairs, scr, out_ref
     )
@@ -465,11 +544,14 @@
     ]
 
 
-def call(body, outs, operands, scratch=(), smem=(), smem_out=(), hbm=(), work=0, limit=24):
+def call(body, outs, operands, scratch=(), smem=(), smem_out=(), hbm=(), hbm_out=(), work=0, limit=24):
     spaces = [
         pltpu.SMEM if i in smem else pltpu.HBM if i in hbm else pltpu.VMEM for i in range(len(operands))
     ]
-    out_spaces = [pltpu.SMEM if i in smem_out else pltpu.VMEM for i in range(len(outs))]
+    out_spaces = [
+        pltpu.SMEM if i in smem_out else pltpu.HBM if i in hbm_out else pltpu.VMEM
+        for i in range(len(outs))
+    ]
     return pl.pallas_call(
         body,
         out_shape=[jax.ShapeDtypeStruct(shape, dtype) for shape, dtype in outs],
@@ -536,9 +618,10 @@
         work=coarse_work,
     )
     recv = exchange(send, "src")
-    right, ln, rn, tgt_weights, first_rows = call(
+    left, right, ln, rn, tgt_weights, first_rows = call(
         coarse_rows_first,
         [
+            (src_centroids.shape, bf16),
             ((ct, LANES), bf16),
             ((csr, LANES), f32),
             ((ctr, LANES), f32),
@@ -552,7 +635,7 @@
     send, coarse_tgt = call(
         coarse_rows_second,
         [((n_tgt, 2 * csr, LANES), f32), ((ctr, LANES), f32)],
-        [recv, first_rows, src_centroids, right, ln, rn, tgt_weights],
+        [recv, first_rows, left, right, ln, rn, tgt_weights],
         coarse_scratch + [one(csr)],
         work=coarse_work,
     )
@@ -563,7 +646,7 @@
             ((ft, LANES), bf16),
             ((fsr, LANES), f32),
             ((ftr, LANES), f32),
-            ((2 * room + 1,), jnp.int32),
+            ((2 * room + 2,), jnp.int32),
         ],
         [src_cells, tgt_cells, support, counts, coarse_tgt],
         smem=(2, 3),
@@ -571,41 +654,59 @@
         work=2 * coarse_work,
     )
     recv = exchange(send, "tgt")
-    (send,) = call(
+    send, done = call(
         coarse_cols,
-        [((n_src, csr + ctr, LANES), f32)],
-        [recv, src_centroids, right, ln, rn, src_weights, fine_rn],
+        [((n_src, csr + ctr, LANES), f32), ((1, LANES), f32)],
+        [recv, left, right, ln, rn, src_weights, fine_rn],
         coarse_scratch + [one(ctr)],
         work=coarse_work,
     )
     every_src = exchange(send, "src")
-    (send,) = call(coarse_end, [((n_tgt, ctr, LANES), f32)], [every_src, coarse_tgt])
+    held = (CHUNKS * CHUNK, TILE, TILE)
+    holding = [pltpu.VMEM(held, f32), pltpu.SemaphoreType.DMA((CHUNKS,))]
+    stored, done = call(
+        store_some,
+        [(held, f32), ((1, LANES), f32)],
+        [listed, src_cells, fine_right, done],
+        holding,
+        smem=(0,),
+        hbm_out=(0,),
+        limit=48,
+        work=fine_work // 2,
+    )
+    (send,) = call(coarse_end, [((n_tgt, ctr, LANES), f32)], [every_src, coarse_tgt, done])
     every_tgt = exchange(send, "tgt")
 
     fine_static = [src_cells, fine_right, fine_ln, fine_rn]
     send, fine_src = call(
         fine_cols_first,
         [((n_src, ftr, LANES), f32), ((fsr, LANES), f32)],
-        [listed, every_src, src_cluster, *fine_static, src_mass],
-        fine_scratch + [one(n_src * csr), one(ftr)],
+        [listed, stored, every_src, src_cluster, *fine_static, src_mass],
+        fine_scratch + [one(n_src * csr), one(ftr)] + holding,
         smem=(0,),
+        hbm=(1,),
+        limit=48,
         work=fine_work,
     )
     recv = exchange(send, "src")
     first_rows, fine_tgt = call(
         fine_rows_first,
         [((fsr, LANES), f32), ((ftr, LANES), f32)],
-        [listed, every_tgt, tgt_cluster, *fine_static, tgt_mass],
-        fine_scratch + [one(n_tgt * ctr)],
+        [listed, stored, every_tgt, tgt_cluster, *fine_static, tgt_mass],
+        fine_scratch + [one(n_tgt * ctr)] + holding,
         smem=(0,),
+        hbm=(1,),
+        limit=48,
         work=fine_work,
     )
     send, fine_tgt = call(
         fine_rows_second,
         [((n_tgt, 2 * fsr // n_tgt, LANES), f32), ((ftr, LANES), f32)],
-        [listed, recv, fine_tgt, first_rows, *fine_static, tgt_mass],
-        fine_scratch + [one(fsr)],
+        [listed, stored, recv, fine_tgt, first_rows, *fine_static, tgt_mass],
+        fine_scratch + [one(fsr)] + holding,
         smem=(0,),
+        hbm=(1,),
+        limit=48,
         work=fine_work,
     )
     recv = exchange(send, "tgt")
@@ -614,9 +715,11 @@
     (send,) = call(
         fine_cols_second,
         [((n_src, ftr, LANES), f32)],
-        [listed, rows, fine_src, *fine_static, src_mass],
-        fine_scratch + [one(fsr), one(ftr)],
+        [listed, stored, rows, fine_src, *fine_static, src_mass],
+        fine_scratch + [one(fsr), one(ftr)] + holding,
         smem=(0,),
+        hbm=(1,),
+        limit=48,
         work=fine_work,
     )
     recv = exchange(send, "src")

time: 294 us -> 307 us (1.044)
  the two profiles are of different devices: /device:TPU:195 before, /device:TPU:261 now
where the time goes in v4:
time: 307 us; the launch traced here: 306 us
  blocking collectives  127 us (41%)
  Pallas kernels  97 us (32%)
  starting transfers between devices  62.3 us (20%)
  local copies, waits for them, and re-layouts  9.53 us (3%)
  waiting for transfers between devices  9.29 us (3%)
    all_to_all x3, blocking collectives, exchange(): return lax.all_to_all(x, axis, 0, 0, tiled=True)  127 us
    pallas_call x13, Pallas kernels, call(): pl.pallas_call(body, out_shape=[jax.ShapeDtypeStruct(shape, dtype) for sh...  97 us
    all_to_all x5, starting transfers between devices, exchange(): return lax.all_to_all(x, axis, 0, 0, tiled=True)  62.3 us
    unnamed x28, local copies, waits for them, and re-layouts  9.53 us
    all_to_all x5, waiting for transfers between devices, exchange(): return lax.all_to_all(x, axis, 0, 0, tiled=True)  9.29 us
  transfers between devices with their start and end apart: 5, of which 3 were waited for; matrix products, arithmetic and copies ran while one was open for 0% of the time, Pallas kernels for 16%

profile of v4, /device:TPU:261, one launch (start us, length us, event | category | flops | bytes accessed | tf_op | source)
XLA Modules:
  0.0 305.5 jit_solution(13468963528491298635)
XLA Ops:
  0.6 3.9 %shard_map.131 = f32[16,4,128]{2,1,0:T(4,128)} custom-call(bf16[64,1024]{1,0:T(8,128)(2,1)} %src_ref.3, bf16[64,512]{1,0:T(8,128)(2,1)} %points_ref.2, f32[8,128]{1,0:T(8,128)} %bitcast.14), custom_call_target="tpu_custom_call" | custom-call | flops 67109864 | bytes 1048576 | tf_op jit(solution)/shard_map/pallas_call | solution.py:555
  4.5 0.0 copy-start.2
  4.5 7.9 %all-to-all-start = ((f32[16,4,128]{2,1,0:T(4,128)}), f32[16,4,128]{2,1,0:T(4,128)S(1)}, u32[]{:S(2)}, u32[]{:S(2)}) async-start(f32[16,4,128]{2,1,0:T(4,128)} %shard_map.131), calls=%async_computation | async-start | bytes 65536 | tf_op jit(solution)/shard_map/all_to_all | solution.py:569
  12.5 0.0 copy-start.9
  12.5 0.9 copy-done.9
  13.4 0.0 copy-start.10
  13.4 0.8 copy-done.10
  14.2 0.0 copy-start.12
  14.2 0.7 copy-done.12
  14.9 2.2 shard_map.132
  17.1 2.7 all-to-all-done.recv_ref
  19.9 3.0 shard_map.133
  22.8 0.0 copy-start.6
  22.8 0.0 copy-start.7
  22.8 9.4 %all-to-all-start.1 = ((f32[32,16,128]{2,1,0:T(8,128)}), f32[32,16,128]{2,1,0:T(8,128)S(1)}, u32[]{:S(2)}, u32[]{:S(2)}) async-start(f32[32,16,128]{2,1,0:T(8,128)} %get-tuple-element.35), calls=%async_computation.1 | async-start | bytes 524288 | tf_op jit(solution)/shard_map/all_to_all | solution.py:569
  32.2 0.8 copy.14.support_ref
  33.0 0.7 copy.15.counts_ref
  33.7 0.0 copy-start
  33.7 1.2 copy-done
  34.9 0.0 copy-start.8
  34.9 0.9 copy-done.8
  35.9 2.3 shard_map.134
  38.2 1.0 all-to-all-done.1.recv_ref
  39.2 0.0 copy-start.11
  39.2 0.7 copy-done.11
  39.9 3.1 %shard_map.135 = (f32[16,12,128]{2,1,0:T(8,128)}, f32[1,128]{1,0:T(1,128)S(1)}) custom-call(f32[32,16,128]{2,1,0:T(8,128)S(1)} %all-to-all-done.1.recv_ref, bf16[64,1024]{1,0:T(8,128)(2,1)S(1)} %get-tuple-element.27.left_ref, bf16[512,128]{1,0:T(8,128)(2,1)S(1)} %get-tuple-element.28.right_ref, f32[8,128]{1,0:T(8,128)S(1)} %get-tuple-element.29.ln_ref, ...), custom_call_target="tpu_custom_call" | custom-call | flops 67109864 | bytes 1048576 | tf_op jit(solution)/shard_map/pallas_call | solution.py:555
  42.9 5.4 %all-to-all-start.2 = ((f32[16,12,128]{2,1,0:T(8,128)}), f32[16,12,128]{2,1,0:T(8,128)S(1)}, u32[]{:S(2)}, u32[]{:S(2)}) async-start(f32[16,12,128]{2,1,0:T(8,128)} %get-tuple-element.39), calls=%async_computation.2 | async-start | bytes 262144 | tf_op jit(solution)/shard_map/all_to_all | solution.py:569
  48.3 0.0 copy-start.1
  48.3 1.2 copy-done.1
  49.6 2.4 shard_map.136
  51.9 5.6 %all-to-all-done.2.recv_ref = f32[16,12,128]{2,1,0:T(8,128)S(1)} async-done(((f32[16,12,128]{2,1,0:T(8,128)}), f32[16,12,128]{2,1,0:T(8,128)S(1)}, u32[]{:S(2)}, u32[]{:S(2)}) %all-to-all-start.2) | async-done | bytes 98336 | tf_op jit(solution)/shard_map/all_to_all | solution.py:569
  57.5 0.7 shard_map.138
  58.2 9.3 %all-to-all-start.4 = ((f32[32,4,128]{2,1,0:T(4,128)}), f32[32,4,128]{2,1,0:T(4,128)S(1)}, u32[]{:S(2)}, u32[]{:S(2)}) async-start(f32[32,4,128]{2,1,0:T(4,128)} %shard_map.138), calls=%async_computation.4 | async-start | bytes 131072 | tf_op jit(solution)/shard_map/all_to_all | solution.py:569
  67.5 0.0 copy-done.2
  67.5 0.0 copy-start.3
  67.5 0.7 copy-done.3
  68.3 0.0 copy-start.5
  68.3 0.8 copy-done.5
  69.1 21.6 %shard_map.137 = (f32[16,16,128]{2,1,0:T(8,128)}, f32[64,128]{1,0:T(8,128)S(1)}) custom-call(s32[290]{0:T(512)S(1)} %get-tuple-element.33.list_ref, f32[40,256,256]{2,1,0:T(8,128)} %get-tuple-element.38.stored_ref, f32[16,12,128]{2,1,0:T(8,128)S(1)} %all-to-all-done.2.recv_ref, s32[64,128]{1,0:T(8,128)S(1)} %bitcast.10, bf16[64,8192]{1,0:T(8,128)(2,1)S(1)} %copy-done.2, ...), custom_call_target="tpu_custom_call" | custom-call | flops 536871936 | bytes 1048576 | tf_op jit(solution)/shard_map/pallas_call | solution.py:555
  90.7 0.0 all-to-all-done.4.recv_ref
  90.7 30.3 %all-to-all-start.3 = ((f32[16,16,128]{2,1,0:T(8,128)}), f32[16,16,128]{2,1,0:T(8,128)S(1)}, u32[]{:S(2)}, u32[]{:S(2)}) async-start(f32[16,16,128]{2,1,0:T(8,128)} %get-tuple-element.41), calls=%async_computation.3 | async-start | bytes 262144 | tf_op jit(solution)/shard_map/all_to_all | solution.py:569
  121.0 0.0 copy-done.6
  121.0 0.0 copy-done.7
  121.0 0.0 copy-start.4
  121.0 19.2 %shard_map.139 = (f32[64,128]{1,0:T(8,128)S(1)}, f32[16,128]{1,0:T(8,128)S(1)}) custom-call(s32[290]{0:T(512)S(1)} %get-tuple-element.33.list_ref, f32[40,256,256]{2,1,0:T(8,128)} %get-tuple-element.38.stored_ref, f32[32,4,128]{2,1,0:T(4,128)S(1)} %all-to-all-done.4.recv_ref, s32[16,128]{1,0:T(8,128)S(1)} %bitcast.13, bf16[64,8192]{1,0:T(8,128)(2,1)S(1)} %copy-done.2, ...), custom_call_target="tpu_custom_call" | custom-call | flops 536871936 | bytes 1048576 | tf_op jit(solution)/shard_map/pallas_call | solution.py:555
  140.2 0.0 all-to-all-done.3.recv_ref
  140.2 19.0 %shard_map.140 = (f32[32,4,128]{2,1,0:T(4,128)S(1)}, f32[16,128]{1,0:T(8,128)S(1)}) custom-call(s32[290]{0:T(512)S(1)} %get-tuple-element.33.list_ref, f32[40,256,256]{2,1,0:T(8,128)} %get-tuple-element.38.stored_ref, f32[16,16,128]{2,1,0:T(8,128)S(1)} %all-to-all-done.3.recv_ref, f32[16,128]{1,0:T(8,128)S(1)} %get-tuple-element.43.tgt_ref, ...), custom_call_target="tpu_custom_call" | custom-call | flops 536871936 | bytes 1048576 | tf_op jit(solution)/shard_map/pallas_call | solution.py:555
  159.2 58.0 %all_to_all.40.recv_ref = f32[32,4,128]{2,1,0:T(4,128)S(1)} all-to-all(f32[32,4,128]{2,1,0:T(4,128)S(1)} %get-tuple-element.45), channel_id=1, replica_groups=mesh['src'=16,'tgt'=32] {'tgt'}, dimensions={0} | all-to-all | bytes 131072 | tf_op jit(solution)/shard_map/all_to_all | solution.py:569
  217.3 0.1 shard_map.141
  217.3 12.0 %all_to_all.41.recv_ref.rows_ref = f32[32,4,128]{2,1,0:T(4,128)S(1)} all-to-all(f32[32,4,128]{2,1,0:T(4,128)S(1)} %shard_map.141), channel_id=1, replica_groups=mesh['src'=16,'tgt'=32] {'tgt'}, dimensions={0} | all-to-all | bytes 131072 | tf_op jit(solution)/shard_map/all_to_all | solution.py:569
  229.4 0.0 copy-done.4
  229.4 18.9 %shard_map.142 = f32[16,16,128]{2,1,0:T(8,128)S(1)} custom-call(s32[290]{0:T(512)S(1)} %get-tuple-element.33.list_ref, f32[40,256,256]{2,1,0:T(8,128)} %get-tuple-element.38.stored_ref, f32[32,4,128]{2,1,0:T(4,128)S(1)} %all_to_all.41.recv_ref.rows_ref, f32[64,128]{1,0:T(8,128)S(1)} %get-tuple-element.46.src_ref, bf16[64,8192]{1,0:T(8,128)(2,1)S(1)} %copy-done.2, ...), custom_call_target="tpu_custom_call" | custom-call | flops 536871936 | bytes 1048576 | tf_op jit(solution)/shard_map/pallas_call | solution.py:555
  248.3 56.5 %all_to_all.42.recv_ref = f32[16,16,128]{2,1,0:T(8,128)S(1)} all-to-all(f32[16,16,128]{2,1,0:T(8,128)S(1)} %shard_map.142), channel_id=1, replica_groups=mesh['src'=16,'tgt'=32] {'src'}, dimensions={0} | all-to-all | bytes 262144 | tf_op jit(solution)/shard_map/all_to_all | solution.py:569
  304.8 0.7 shard_map.143
Async XLA Ops:
  4.5 63.0 %copy-start.2 = (bf16[64,8192]{1,0:T(8,128)(2,1)S(1)}, bf16[64,8192]{1,0:T(8,128)(2,1)}, u32[]{:S(2)}) copy-start(bf16[64,8192]{1,0:T(8,128)(2,1)} %left_ref.11) | copy-start | bytes 3145732
  4.5 15.3 %all-to-all-start = ((f32[16,4,128]{2,1,0:T(4,128)}), f32[16,4,128]{2,1,0:T(4,128)S(1)}, u32[]{:S(2)}, u32[]{:S(2)}) async-start(f32[16,4,128]{2,1,0:T(4,128)} %shard_map.131), calls=%async_computation | async-start | bytes 65536 | tf_op jit(solution)/shard_map/all_to_all | solution.py:569
  12.5 0.9 copy-start.9
  13.4 0.8 copy-start.10
  14.2 0.7 copy-start.12
  22.8 98.1 %copy-start.6 = (f32[2048]{0:T(1024)S(1)}, f32[2048]{0:T(1024)}, u32[]{:S(2)}) copy-start(f32[2048]{0:T(1024)} %param.19) | copy-start | bytes 24580
  22.8 98.1 %copy-start.7 = (s32[2048]{0:T(1024)S(1)}, s32[2048]{0:T(1024)}, u32[]{:S(2)}) copy-start(s32[2048]{0:T(1024)} %param.21) | copy-start | bytes 24580
  22.8 16.3 %all-to-all-start.1 = ((f32[32,16,128]{2,1,0:T(8,128)}), f32[32,16,128]{2,1,0:T(8,128)S(1)}, u32[]{:S(2)}, u32[]{:S(2)}) async-start(f32[32,16,128]{2,1,0:T(8,128)} %get-tuple-element.35), calls=%async_computation.1 | async-start | bytes 524288 | tf_op jit(solution)/shard_map/all_to_all | solution.py:569
  33.7 1.2 copy-start
  34.9 0.9 copy-start.8
  39.2 0.7 copy-start.11
  42.9 14.6 %all-to-all-start.2 = ((f32[16,12,128]{2,1,0:T(8,128)}), f32[16,12,128]{2,1,0:T(8,128)S(1)}, u32[]{:S(2)}, u32[]{:S(2)}) async-start(f32[16,12,128]{2,1,0:T(8,128)} %get-tuple-element.39), calls=%async_computation.2 | async-start | bytes 262144 | tf_op jit(solution)/shard_map/all_to_all | solution.py:569
  48.3 1.2 copy-start.1
  58.2 32.5 %all-to-all-start.4 = ((f32[32,4,128]{2,1,0:T(4,128)}), f32[32,4,128]{2,1,0:T(4,128)S(1)}, u32[]{:S(2)}, u32[]{:S(2)}) async-start(f32[32,4,128]{2,1,0:T(4,128)} %shard_map.138), calls=%async_computation.4 | async-start | bytes 131072 | tf_op jit(solution)/shard_map/all_to_all | solution.py:569
  67.5 0.8 copy-start.3
  68.3 0.8 copy-start.5
  90.7 49.5 %all-to-all-start.3 = ((f32[16,16,128]{2,1,0:T(8,128)}), f32[16,16,128]{2,1,0:T(8,128)S(1)}, u32[]{:S(2)}, u32[]{:S(2)}) async-start(f32[16,16,128]{2,1,0:T(8,128)} %get-tuple-element.41), calls=%async_computation.3 | async-start | bytes 262144 | tf_op jit(solution)/shard_map/all_to_all | solution.py:569
  121.0 108.4 %copy-start.4 = (f32[8192]{0:T(1024)S(1)}, f32[8192]{0:T(1024)}, u32[]{:S(2)}) copy-start(f32[8192]{0:T(1024)} %param.18) | copy-start | bytes 98308

commit v5 on v3

--- a/solution.py
+++ b/solution.py
@@ -302,8 +302,9 @@
 
 
 def coarse_rows_first(
-    left_ref, points_ref, from_ref, right_ref, ln_ref, rn_ref, weight_ref, out_ref, *scr
-):
+    src_ref, points_ref, from_ref, left_ref, right_ref, ln_ref, rn_ref, weight_ref, out_ref, *scr
+):
+    left_ref[...] = src_ref[...]
     prepare_points(left_ref, points_ref, right_ref, ln_ref, rn_ref)
     weight = from_ref[...]
     weight_ref[...] = weight
@@ -536,9 +537,10 @@
         work=coarse_work,
     )
     recv = exchange(send, "src")
-    right, ln, rn, tgt_weights, first_rows = call(
+    left, right, ln, rn, tgt_weights, first_rows = call(
         coarse_rows_first,
         [
+            (src_centroids.shape, bf16),
             ((ct, LANES), bf16),
             ((csr, LANES), f32),
             ((ctr, LANES), f32),
@@ -552,7 +554,7 @@
     send, coarse_tgt = call(
         coarse_rows_second,
         [((n_tgt, 2 * csr, LANES), f32), ((ctr, LANES), f32)],
-        [recv, first_rows, src_centroids, right, ln, rn, tgt_weights],
+        [recv, first_rows, left, right, ln, rn, tgt_weights],
         coarse_scratch + [one(csr)],
         work=coarse_work,
     )
@@ -574,7 +576,7 @@
     (send,) = call(
         coarse_cols,
         [((n_src, csr + ctr, LANES), f32)],
-        [recv, src_centroids, right, ln, rn, src_weights, fine_rn],
+        [recv, left, right, ln, rn, src_weights, fine_rn],
         coarse_scratch + [one(ctr)],
         work=coarse_work,
     )

time: 294 us -> 296 us (level)
  the two profiles are of different devices: /device:TPU:195 before, /device:TPU:1 now
where the time goes in v5:
time: 296 us; the launch traced here: 298 us
  blocking collectives  158 us (53%)
  Pallas kernels  77.1 us (26%)
  starting transfers between devices  48.1 us (16%)
  waiting for transfers between devices  11.8 us (4%)
    all_to_all x4, blocking collectives, exchange(): return lax.all_to_all(x, axis, 0, 0, tiled=True)  158 us
    pallas_call x12, Pallas kernels, call(): pl.pallas_call(body, out_shape=[jax.ShapeDtypeStruct(shape, dtype) for sh...  77.1 us
    all_to_all x4, starting transfers between devices, exchange(): return lax.all_to_all(x, axis, 0, 0, tiled=True)  48.1 us
    all_to_all x4, waiting for transfers between devices, exchange(): return lax.all_to_all(x, axis, 0, 0, tiled=True)  11.8 us
  transfers between devices with their start and end apart: 4, of which 2 were waited for; matrix products, arithmetic and copies ran while one was open for 0% of the time, Pallas kernels for 20%

profile of v5, /device:TPU:1, one launch (start us, length us, event | category | flops | bytes accessed | tf_op | source)
XLA Modules:
  0.0 298.2 jit_solution(9836509746531853865)
XLA Ops:
  0.6 2.3 shard_map.131
  2.9 0.0 copy-start.3
  3.0 10.3 %all-to-all-start = ((f32[16,4,128]{2,1,0:T(4,128)}), f32[16,4,128]{2,1,0:T(4,128)S(1)}, u32[]{:S(2)}, u32[]{:S(2)}) async-start(f32[16,4,128]{2,1,0:T(4,128)} %shard_map.131), calls=%async_computation | async-start | bytes 65536 | tf_op jit(solution)/shard_map/all_to_all | solution.py:488
  13.3 0.0 copy-done.3
  13.3 0.0 copy-start.2
  13.3 0.9 copy-done.2
  14.2 0.0 copy-start.9
  14.2 0.7 copy-done.9
  14.9 0.0 copy-start
  14.9 0.7 shard_map.132
  15.6 5.1 %all-to-all-done.recv_ref = f32[16,4,128]{2,1,0:T(4,128)S(1)} async-done(((f32[16,4,128]{2,1,0:T(4,128)}), f32[16,4,128]{2,1,0:T(4,128)S(1)}, u32[]{:S(2)}, u32[]{:S(2)}) %all-to-all-start) | async-done | bytes 32800 | tf_op jit(solution)/shard_map/all_to_all | solution.py:488
  20.7 3.0 %shard_map.133 = (f32[32,16,128]{2,1,0:T(8,128)}, f32[4,128]{1,0:T(4,128)S(1)}) custom-call(f32[16,4,128]{2,1,0:T(4,128)S(1)} %all-to-all-done.recv_ref, f32[8,128]{1,0:T(8,128)S(1)} %get-tuple-element.22.first_ref, bf16[64,1024]{1,0:T(8,128)(2,1)S(1)} %get-tuple-element.23.left_ref, bf16[512,128]{1,0:T(8,128)(2,1)S(1)} %get-tuple-element.24.right_ref, ...), custom_call_target="tpu_custom_call" | custom-call | flops 67109864 | bytes 1048576 | tf_op jit(solution)/shard_map/pallas_call | solution.py:474
  23.7 0.0 copy-start.10
  23.7 0.0 copy-start.1
  23.7 12.7 %all-to-all-start.1 = ((f32[32,16,128]{2,1,0:T(8,128)}), f32[32,16,128]{2,1,0:T(8,128)S(1)}, u32[]{:S(2)}, u32[]{:S(2)}) async-start(f32[32,16,128]{2,1,0:T(8,128)} %get-tuple-element.30), calls=%async_computation.1 | async-start | bytes 524288 | tf_op jit(solution)/shard_map/all_to_all | solution.py:488
  36.5 0.0 copy-done.10
  36.5 0.0 copy-start.11
  36.5 0.1 copy.14.support_ref
  36.6 0.6 copy-done.11
  37.1 0.1 copy.15.counts_ref
  37.2 0.0 copy-done
  37.2 0.0 copy-done.1
  37.2 0.0 copy-start.8
  37.2 2.3 shard_map.134
  39.5 6.6 %all-to-all-done.1.recv_ref = f32[32,16,128]{2,1,0:T(8,128)S(1)} async-done(((f32[32,16,128]{2,1,0:T(8,128)}), f32[32,16,128]{2,1,0:T(8,128)S(1)}, u32[]{:S(2)}, u32[]{:S(2)}) %all-to-all-start.1) | async-done | bytes 262176 | tf_op jit(solution)/shard_map/all_to_all | solution.py:488
  46.1 0.0 copy-done.8
  46.1 2.4 shard_map.135
  48.6 14.6 %all_to_all.40.recv_ref = f32[16,12,128]{2,1,0:T(8,128)S(1)} all-to-all(f32[16,12,128]{2,1,0:T(8,128)S(1)} %shard_map.135), channel_id=1, replica_groups=mesh['src'=16,'tgt'=32] {'src'}, dimensions={0} | all-to-all | bytes 196608 | tf_op jit(solution)/shard_map/all_to_all | solution.py:488
  63.2 0.7 shard_map.137
  63.8 0.0 copy-start.4
  63.8 0.0 copy-start.5
  63.8 5.1 %all-to-all-start.4 = ((f32[32,4,128]{2,1,0:T(4,128)}), f32[32,4,128]{2,1,0:T(4,128)S(1)}, u32[]{:S(2)}, u32[]{:S(2)}) async-start(f32[32,4,128]{2,1,0:T(4,128)} %shard_map.137), calls=%async_computation.4 | async-start | bytes 131072 | tf_op jit(solution)/shard_map/all_to_all | solution.py:488
  69.0 0.0 copy-done.4
  69.0 0.0 copy-done.5
  69.0 29.6 %shard_map.136 = (f32[16,16,128]{2,1,0:T(8,128)}, f32[64,128]{1,0:T(8,128)S(1)}) custom-call(s32[289]{0:T(512)S(1)} %get-tuple-element.29.list_ref, f32[16,12,128]{2,1,0:T(8,128)S(1)} %all_to_all.40.recv_ref, s32[64,128]{1,0:T(8,128)S(1)} %bitcast.8, bf16[64,8192]{1,0:T(8,128)(2,1)S(1)} %copy-done, bf16[2048,128]{1,0:T(8,128)(2,1)S(1)} %get-tuple-element.32.right_ref, ...), custom_call_target="tpu_custom_call" | custom-call | flops 536871936 | bytes 1048576 | tf_op jit(solution)/shard_map/pallas_call | solution.py:474
  98.5 0.0 all-to-all-done.4.recv_ref
  98.5 0.0 copy-start.6
  98.5 0.0 copy-start.7
  98.6 20.0 %all-to-all-start.3 = ((f32[16,16,128]{2,1,0:T(8,128)}), f32[16,16,128]{2,1,0:T(8,128)S(1)}, u32[]{:S(2)}, u32[]{:S(2)}) async-start(f32[16,16,128]{2,1,0:T(8,128)} %get-tuple-element.34), calls=%async_computation.3 | async-start | bytes 262144 | tf_op jit(solution)/shard_map/all_to_all | solution.py:488
  118.6 0.0 copy-done.6
  118.6 0.0 copy-done.7
  118.6 26.8 %shard_map.138 = (f32[64,128]{1,0:T(8,128)S(1)}, f32[16,128]{1,0:T(8,128)S(1)}) custom-call(s32[289]{0:T(512)S(1)} %get-tuple-element.29.list_ref, f32[32,4,128]{2,1,0:T(4,128)S(1)} %all-to-all-done.4.recv_ref, s32[16,128]{1,0:T(8,128)S(1)} %bitcast.11, bf16[64,8192]{1,0:T(8,128)(2,1)S(1)} %copy-done, bf16[2048,128]{1,0:T(8,128)(2,1)S(1)} %get-tuple-element.32.right_ref, ...), custom_call_target="tpu_custom_call" | custom-call | flops 536871936 | bytes 1048576 | tf_op jit(solution)/shard_map/pallas_call | solution.py:474
  145.4 0.0 all-to-all-done.3.recv_ref
  145.4 4.3 %shard_map.139 = (f32[32,4,128]{2,1,0:T(4,128)S(1)}, f32[16,128]{1,0:T(8,128)S(1)}) custom-call(s32[289]{0:T(512)S(1)} %get-tuple-element.29.list_ref, f32[16,16,128]{2,1,0:T(8,128)S(1)} %all-to-all-done.3.recv_ref, f32[16,128]{1,0:T(8,128)S(1)} %get-tuple-element.35.tgt_ref, f32[64,128]{1,0:T(8,128)S(1)} %get-tuple-element.36.first_ref, ...), custom_call_target="tpu_custom_call" | custom-call | flops 536871936 | bytes 1048576 | tf_op jit(solution)/shard_map/pallas_call | solution.py:474
  149.7 72.9 %all_to_all.41.recv_ref = f32[32,4,128]{2,1,0:T(4,128)S(1)} all-to-all(f32[32,4,128]{2,1,0:T(4,128)S(1)} %get-tuple-element.37), channel_id=1, replica_groups=mesh['src'=16,'tgt'=32] {'tgt'}, dimensions={0} | all-to-all | bytes 131072 | tf_op jit(solution)/shard_map/all_to_all | solution.py:488
  222.5 0.1 shard_map.140
  222.6 11.8 %all_to_all.42.recv_ref.rows_ref = f32[32,4,128]{2,1,0:T(4,128)S(1)} all-to-all(f32[32,4,128]{2,1,0:T(4,128)S(1)} %shard_map.140), channel_id=1, replica_groups=mesh['src'=16,'tgt'=32] {'tgt'}, dimensions={0} | all-to-all | bytes 131072 | tf_op jit(solution)/shard_map/all_to_all | solution.py:488
  234.4 4.3 %shard_map.141 = f32[16,16,128]{2,1,0:T(8,128)S(1)} custom-call(s32[289]{0:T(512)S(1)} %get-tuple-element.29.list_ref, f32[32,4,128]{2,1,0:T(4,128)S(1)} %all_to_all.42.recv_ref.rows_ref, f32[64,128]{1,0:T(8,128)S(1)} %get-tuple-element.38.src_ref, bf16[64,8192]{1,0:T(8,128)(2,1)S(1)} %copy-done, bf16[2048,128]{1,0:T(8,128)(2,1)S(1)} %get-tuple-element.32.right_ref, ...), custom_call_target="tpu_custom_call" | custom-call | flops 536871936 | bytes 1048576 | tf_op jit(solution)/shard_map/pallas_call | solution.py:474
  238.7 58.9 %all_to_all.43.recv_ref = f32[16,16,128]{2,1,0:T(8,128)S(1)} all-to-all(f32[16,16,128]{2,1,0:T(8,128)S(1)} %shard_map.141), channel_id=1, replica_groups=mesh['src'=16,'tgt'=32] {'src'}, dimensions={0} | all-to-all | bytes 262144 | tf_op jit(solution)/shard_map/all_to_all | solution.py:488
  297.6 0.7 shard_map.142
Async XLA Ops:
  2.9 10.3 %copy-start.3 = (bf16[64,512]{1,0:T(8,128)(2,1)S(1)}, bf16[64,512]{1,0:T(8,128)(2,1)}, u32[]{:S(2)}) copy-start(bf16[64,512]{1,0:T(8,128)(2,1)} %points_ref.2) | copy-start | bytes 196612
  3.0 17.8 %all-to-all-start = ((f32[16,4,128]{2,1,0:T(4,128)}), f32[16,4,128]{2,1,0:T(4,128)S(1)}, u32[]{:S(2)}, u32[]{:S(2)}) async-start(f32[16,4,128]{2,1,0:T(4,128)} %shard_map.131), calls=%async_computation | async-start | bytes 65536 | tf_op jit(solution)/shard_map/all_to_all | solution.py:488
  13.3 0.9 copy-start.2
  14.2 0.7 copy-start.9
  14.9 22.4 %copy-start = (bf16[64,8192]{1,0:T(8,128)(2,1)S(1)}, bf16[64,8192]{1,0:T(8,128)(2,1)}, u32[]{:S(2)}) copy-start(bf16[64,8192]{1,0:T(8,128)(2,1)} %left_ref.9) | copy-start | bytes 3145732
  23.7 12.7 %copy-start.10 = (s32[32,1,4]{0,2,1:T(4,128)S(1)}, s32[32,1,4]{0,2,1:T(4,128)}, u32[]{:S(2)}) copy-start(s32[32,1,4]{0,2,1:T(4,128)} %param.22) | copy-start | bytes 1540
  23.7 13.5 %copy-start.1 = (bf16[64,2048]{1,0:T(8,128)(2,1)S(1)}, bf16[64,2048]{1,0:T(8,128)(2,1)}, u32[]{:S(2)}) copy-start(bf16[64,2048]{1,0:T(8,128)(2,1)} %points_ref.3) | copy-start | bytes 786436
  23.7 22.4 %all-to-all-start.1 = ((f32[32,16,128]{2,1,0:T(8,128)}), f32[32,16,128]{2,1,0:T(8,128)S(1)}, u32[]{:S(2)}, u32[]{:S(2)}) async-start(f32[32,16,128]{2,1,0:T(8,128)} %get-tuple-element.30), calls=%async_computation.1 | async-start | bytes 524288 | tf_op jit(solution)/shard_map/all_to_all | solution.py:488
  36.5 0.7 copy-start.11
  37.2 8.9 %copy-start.8 = (f32[1024]{0:T(1024)S(1)}, f32[1024]{0:T(1024)}, u32[]{:S(2)}) copy-start(f32[1024]{0:T(1024)} %param.14) | copy-start | bytes 12292
  63.8 5.1 %copy-start.4 = (s32[8192]{0:T(1024)S(1)}, s32[8192]{0:T(1024)}, u32[]{:S(2)}) copy-start(s32[8192]{0:T(1024)} %param.20) | copy-start | bytes 98308
  63.8 5.1 %copy-start.5 = (f32[8192]{0:T(1024)S(1)}, f32[8192]{0:T(1024)}, u32[]{:S(2)}) copy-start(f32[8192]{0:T(1024)} %param.18) | copy-start | bytes 98308
  63.8 34.7 %all-to-all-start.4 = ((f32[32,4,128]{2,1,0:T(4,128)}), f32[32,4,128]{2,1,0:T(4,128)S(1)}, u32[]{:S(2)}, u32[]{:S(2)}) async-start(f32[32,4,128]{2,1,0:T(4,128)} %shard_map.137), calls=%async_computation.4 | async-start | bytes 131072 | tf_op jit(solution)/shard_map/all_to_all | solution.py:488
  98.5 20.0 %copy-start.6 = (s32[2048]{0:T(1024)S(1)}, s32[2048]{0:T(1024)}, u32[]{:S(2)}) copy-start(s32[2048]{0:T(1024)} %param.21) | copy-start | bytes 24580
  98.5 20.0 %copy-start.7 = (f32[2048]{0:T(1024)S(1)}, f32[2048]{0:T(1024)}, u32[]{:S(2)}) copy-start(f32[2048]{0:T(1024)} %param.19) | copy-start | bytes 24580
  98.6 46.8 %all-to-all-start.3 = ((f32[16,16,128]{2,1,0:T(8,128)}), f32[16,16,128]{2,1,0:T(8,128)S(1)}, u32[]{:S(2)}, u32[]{:S(2)}) async-start(f32[16,16,128]{2,1,0:T(8,128)} %get-tuple-element.34), calls=%async_computation.3 | async-start | bytes 262144 | tf_op jit(solution)/shard_map/all_to_all | solution.py:488
